TPU v7x, 256 devices: a whole 4x4x8 slice. The times are simulated.
256 devices in a mesh: row: 16 (over z, core), col: 4 (over y), depth: 4 (over x).
Axes of the slice: x: 4, y: 4, z: 8, core: 2. Of those that a mesh axis runs over, the one named last changes fastest.
Arguments:
- inputs: bfloat16 [8, 2048, 4096], P('depth', 'row', 'col'), may hold values from -12 to 12
- w_query: bfloat16 [4096, 2048], P('row', 'col'), may hold values from -0.109375 to 0.109375
- w_key: bfloat16 [4096, 512], P('row', 'col'), may hold values from -0.078125 to 0.078125
- w_value: bfloat16 [4096, 512], P('row', 'col'), may hold values from -0.09375 to 0.09375
- grad_out: bfloat16 [8, 2048, 2048], P('depth', 'row', 'col'), may hold values from -24 to 24
Outputs:
- grad_inputs: bfloat16 [8, 2048, 4096], P('depth', 'row', 'col')
- grad_query: float32 [4096, 2048], P(('row', 'depth'), 'col')
- grad_key: float32 [4096, 512], P(('row', 'depth'), 'col')
- grad_value: float32 [4096, 512], P(('row', 'depth'), 'col')
All inputs are finite; a program needn't handle non-finite values.
Results may differ from a plain program's by a relative error of at most 0.028.
Values may be sent and summed in bfloat16 or wider, within the bound.
A program may use at most 128 MiB of HBM per device.

v0:
```python
import jax
import jax.numpy as jnp
from jax import lax
from jax.sharding import PartitionSpec as P

D = 4096
HEADS = 16
KV_HEADS = 4
HEAD_DIM = 128
LEN = 2048


def body(inputs, w_query, w_key, w_value, grad_out):
    seq_count, local_len, _ = inputs.shape
    token_count = seq_count * local_len
    query_width = w_query.shape[1]
    kv_width = w_key.shape[1]
    kv_local = kv_width // HEAD_DIM
    group_size = HEADS // KV_HEADS
    score_scale = HEAD_DIM ** (-0.5)
    full_inputs = lax.all_gather(inputs, "col", axis=2, tiled=True).reshape(token_count, D)
    w_tile = jnp.concatenate([w_query, w_key, w_value], 1)
    w_full = lax.all_gather(w_tile, "row", axis=0, tiled=True)
    projected = jnp.dot(full_inputs, w_full, preferred_element_type=jnp.float32)
    projected = projected.astype(jnp.bfloat16)
    queries = projected[:, :query_width].reshape(
        seq_count, local_len, kv_local, group_size, HEAD_DIM
    )
    keys = projected[:, query_width : query_width + kv_width].reshape(
        seq_count, local_len, kv_width
    )
    values = projected[:, query_width + kv_width :].reshape(seq_count, local_len, kv_width)
    keys_all, values_all = (
        lax.all_gather(keys, "row", axis=1, tiled=True),
        lax.all_gather(values, "row", axis=1, tiled=True),
    )
    first_pos = lax.axis_index("row") * local_len
    query_pos = first_pos + jnp.arange(local_len, dtype=jnp.int32)
    key_pos = jnp.arange(LEN, dtype=jnp.int32)
    causal = key_pos[None, :] <= query_pos[:, None]
    cot_heads = grad_out.reshape(seq_count, local_len, kv_local, group_size, HEAD_DIM)

    def one_sequence(packed):
        query_seq, key_seq, value_seq, cot_seq = packed
        key_seq = key_seq.reshape(LEN, kv_local, HEAD_DIM)
        value_seq = value_seq.reshape(LEN, kv_local, HEAD_DIM)
        scores = (
            jnp.einsum("qkgd,tkd->kgqt", query_seq, key_seq, preferred_element_type=jnp.float32)
            * score_scale
        )
        scores = jnp.where(causal, scores, -1e30)
        highest = jnp.max(scores, -1, keepdims=True)
        weights = jnp.exp(scores - highest)
        probs = weights / jnp.sum(weights, -1, keepdims=True)
        probs_low = probs.astype(jnp.bfloat16)
        attended = jnp.einsum(
            "kgqt,tkd->qkgd", probs_low, value_seq, preferred_element_type=jnp.float32
        )
        delta = jnp.sum(attended * cot_seq.astype(jnp.float32), -1).transpose(1, 2, 0)[..., None]
        grad_probs = jnp.einsum(
            "qkgd,tkd->kgqt", cot_seq, value_seq, preferred_element_type=jnp.float32
        )
        grad_scores = (probs * (grad_probs - delta)).astype(jnp.bfloat16)
        grad_q = (
            jnp.einsum("kgqt,tkd->qkgd", grad_scores, key_seq, preferred_element_type=jnp.float32)
            * score_scale
        )
        grad_k = (
            jnp.einsum("kgqt,qkgd->tkd", grad_scores, query_seq, preferred_element_type=jnp.float32)
            * score_scale
        )
        grad_v = jnp.einsum(
            "kgqt,qkgd->tkd", probs_low, cot_seq, preferred_element_type=jnp.float32
        )
        return (
            grad_q.astype(jnp.bfloat16),
            grad_k.reshape(LEN, kv_width),
            grad_v.reshape(LEN, kv_width),
        )

    grad_q, key_part, value_part = lax.map(one_sequence, (queries, keys_all, values_all, cot_heads))
    grad_k, grad_v = (
        lax.psum_scatter(key_part, "row", scatter_dimension=1, tiled=True),
        lax.psum_scatter(value_part, "row", scatter_dimension=1, tiled=True),
    )
    grad_rows = jnp.concatenate(
        [
            grad_q.reshape(token_count, query_width),
            grad_k.astype(jnp.bfloat16).reshape(token_count, kv_width),
            grad_v.astype(jnp.bfloat16).reshape(token_count, kv_width),
        ],
        1,
    )
    input_part = lax.dot_general(
        grad_rows, w_full, (((1,), (1,)), ((), ())), preferred_element_type=jnp.float32
    )
    grad_inputs = lax.psum_scatter(
        input_part.reshape(seq_count, local_len, D), "col", scatter_dimension=2, tiled=True
    )
    grad_inputs = grad_inputs.astype(jnp.bfloat16)
    summed = lax.psum_scatter(
        lax.dot_general(
            full_inputs, grad_rows, (((0,), (0,)), ((), ())), preferred_element_type=jnp.float32
        ),
        ("row", "depth"),
        scatter_dimension=0,
        tiled=True,
    )
    return (
        grad_inputs,
        summed[:, :query_width],
        summed[:, query_width : query_width + kv_width],
        summed[:, query_width + kv_width :],
    )


def solution(mesh):
    return jax.shard_map(
        body,
        mesh=mesh,
        in_specs=(
            P("depth", "row", "col"),
            P("row", "col"),
            P("row", "col"),
            P("row", "col"),
            P("depth", "row", "col"),
        ),
        out_specs=(
            P("depth", "row", "col"),
            P(("row", "depth"), "col"),
            P(("row", "depth"), "col"),
            P(("row", "depth"), "col"),
        ),
        check_vma=False,
    )
```

profile of v0, /device:TPU:1, one launch (start us, length us, event | category | flops | bytes accessed | tf_op | source)
XLA Modules:
  0.0 556.4 jit_solution(10927108872247625219)
XLA Ops:
  7.9 1.8 pad_maximum_fusion
  9.8 37.2 %all-gather.7.cloned.1.call-done = bf16[2,128,4096]{2,1,0:T(8,128)(2,1)} async-done(((bf16[2,128,1024]{2,1,0:T(8,128)(2,1)}), bf16[2,128,4096]{2,1,0:T(8,128)(2,1)}) %all-gather.7.cloned.1.call-update) | async-done | bytes 2097168 | tf_op jit(solution)/shard_map/all_gather | solution.py:21
  47.1 48.9 %all-gather.5.cloned.1.call-done = bf16[4096,768]{1,0:T(8,128)(2,1)} async-done(((bf16[256,768]{1,0:T(8,128)(2,1)}), bf16[4096,768]{1,0:T(8,128)(2,1)}) %all-gather.5.cloned.1.call-update) | async-done | bytes 6291472 | tf_op jit(solution)/shard_map/all_gather | solution.py:23
  96.0 5.2 fusion.41
  104.2 35.1 %all-gather.9.cloned.1.call-done = bf16[2,2048,128]{2,1,0:T(8,128)(2,1)} async-done(((bf16[2,128,128]{2,1,0:T(8,128)(2,1)}), bf16[2,2048,128]{2,1,0:T(8,128)(2,1)}) %all-gather.9.cloned.1.call-update) | async-done | bytes 1048592 | tf_op jit(solution)/shard_map/all_gather | solution.py:34
  139.3 39.6 %all-gather.11.cloned.1.call-done = bf16[2,2048,128]{2,1,0:T(8,128)(2,1)} async-done(((bf16[2,128,128]{2,1,0:T(8,128)(2,1)}), bf16[2,2048,128]{2,1,0:T(8,128)(2,1)}) %all-gather.11.cloned.1.call-update) | async-done | bytes 1048592 | tf_op jit(solution)/shard_map/all_gather | solution.py:35
  178.9 32.7 %while.15 = (s32[]{:T(128)}, bf16[2,128,1,4,128]{4,3,1,0,2:T(4,128)(2,1)}, f32[2,2048,128]{2,1,0:T(8,128)}, f32[2,2048,128]{2,1,0:T(8,128)}, bf16[2,2048,128]{2,...) while((s32[]{:T(128)}, ...), condition=%wide.region_4.5_spmd.clone, body=%wide.region_0.4_spmd.clone.sunk | while | flops 1625094656 | bytes 69227224 | solution.py:81
  180.1 1.8 fusion.79
  185.8 1.7 convolution_bitcast_fusion.4
  187.9 3.4 fusion.83
  193.8 1.5 constant_dynamic-update-slice_fusion.6
  196.5 1.8 fusion.79
  202.2 1.7 convolution_bitcast_fusion.4
  204.3 3.4 fusion.83
  212.6 53.7 %reduce-scatter.9.cloned.1.call-done = f32[2,128,128]{2,1,0:T(8,128)} async-done(((f32[2,2048,128]{2,1,0:T(8,128)}), f32[2,128,128]{2,1,0:T(8,128)}) %reduce-scatter.9.cloned.1.call-update) | async-done | bytes 131088 | tf_op jit(solution)/shard_map/reduce_scatter | solution.py:84
  267.3 59.3 %reduce-scatter.7.cloned.1.call-done = f32[2,128,128]{2,1,0:T(8,128)} async-done(((f32[2,2048,128]{2,1,0:T(8,128)}), f32[2,128,128]{2,1,0:T(8,128)}) %reduce-scatter.7.cloned.1.call-update) | async-done | bytes 131088 | tf_op jit(solution)/shard_map/reduce_scatter | solution.py:83
  327.5 6.6 %fusion.42 = f32[256,4096]{1,0:T(8,128)} fusion(bf16[4096,768]{1,0:T(8,128)(2,1)} %all-gather.5.cloned.1.call-done, bf16[256,128]{1,0:T(8,128)(2,1)S(1)} %bitcast.170, bf16[256,128]{1,0:T(8,128)(2,1)S(1)} %bitcast.172, bf16[256,512]{1,0:T(8,128)(2,1)S(1)} %bitcast.168), kind=kOutput, calls=%fused_computation.52 | convolution fusion | flops 1611792384 | bytes 10878976 | tf_op jit(solution)/shard_map/dot_general | solution.py:94
  334.2 1.5 copy-done.3
  335.7 6.3 %convolution_bitcast_fusion.2 = f32[4096,768]{0,1:T(8,128)} fusion(bf16[256,4096]{1,0:T(8,128)(2,1)S(1)} %bitcast.167, bf16[256,128]{1,0:T(8,128)(2,1)S(1)} %bitcast.171, bf16[256,128]{1,0:T(8,128)(2,1)S(1)} %bitcast.173, bf16[256,512]{1,0:T(8,128)(2,1)S(1)} %bitcast.169), kind=kOutput, calls=%fused_computation.46 | convolution fusion | flops 1611792384 | bytes 15073280 | tf_op jit(solution)/shard_map/dot_general | solution.py:102
  342.0 12.7 %copy.69 = f32[4096,768]{1,0:T(8,128)} copy(f32[4096,768]{0,1:T(8,128)} %convolution_bitcast_fusion.2) | data formatting | bytes 25165824
  354.7 30.5 %reduce-scatter.11.cloned.1.call-done = f32[2,128,1024]{2,1,0:T(8,128)} async-done(((f32[2,128,4096]{2,1,0:T(8,128)}), f32[2,128,1024]{2,1,0:T(8,128)}) %reduce-scatter.11.cloned.1.call-update) | async-done | bytes 1048592 | tf_op jit(solution)/shard_map/reduce_scatter | solution.py:97
  385.2 2.1 convert_element_type.48
  387.3 159.3 %reduce-scatter.13.cloned.1.call-done = f32[64,768]{1,0:T(8,128)} async-done(((f32[4096,768]{1,0:T(8,128)}), f32[64,768]{1,0:T(8,128)}) %reduce-scatter.13.cloned.1.call-update) | async-done | bytes 196624
  548.0 1.6 slice.27
  (68 shorter events, 25.2 us)
Async XLA Ops:
  7.2 39.9 %all-gather.7.cloned.1.call-start = ((), (), s32[]{:S(2)}) async-start(), calls=%async_computation.5 | async-start | bytes 2621440 | tf_op jit(solution)/shard_map/all_gather | solution.py:21
  7.9 88.1 %all-gather.5.cloned.1.call-start = ((), (), s32[]{:S(2)}) async-start(), calls=%async_computation.4 | async-start | bytes 6684672 | tf_op jit(solution)/shard_map/all_gather | solution.py:23
  9.8 129.6 %all-gather.9.cloned.1.call-start = ((), (), s32[]{:S(2)}) async-start(), calls=%async_computation.6 | async-start | bytes 1114112 | tf_op jit(solution)/shard_map/all_gather | solution.py:34
  96.0 6.6 %copy-start.4 = (bf16[2,128,512]{2,1,0:T(8,128)(2,1)S(1)}, bf16[2,128,512]{2,1,0:T(8,128)(2,1)}, u32[]{:S(2)}) copy-start(bf16[2,128,512]{2,1,0:T(8,128)(2,1)} %param.11) | copy-start | bytes 786436
  101.9 77.0 %all-gather.11.cloned.1.call-start = ((), (), s32[]{:S(2)}) async-start(), calls=%async_computation.7 | async-start | bytes 1114112 | tf_op jit(solution)/shard_map/all_gather | solution.py:35
  102.5 163.9 %reduce-scatter.9.cloned.1.call-start = ((), (), s32[]{:S(2)}) async-start(), calls=%async_computation.9 | async-start | bytes 2228224 | tf_op jit(solution)/shard_map/reduce_scatter | solution.py:84
  181.9 2.0 copy-start
  182.4 2.0 copy-start.2
  187.9 3.4 copy-start.1
  198.2 2.0 copy-start
  198.8 2.0 copy-start.2
  204.3 3.4 copy-start.1
  211.7 0.9 copy-start.5
  211.7 114.9 %reduce-scatter.7.cloned.1.call-start = ((), (), s32[]{:S(2)}) async-start(), calls=%async_computation.8 | async-start | bytes 2228224 | tf_op jit(solution)/shard_map/reduce_scatter | solution.py:83
  212.3 172.9 %reduce-scatter.11.cloned.1.call-start = ((), (), s32[]{:S(2)}) async-start(), calls=%async_computation.10 | async-start | bytes 5242880 | tf_op jit(solution)/shard_map/reduce_scatter | solution.py:97
  334.1 1.6 copy-start.3
  334.1 212.5 %reduce-scatter.13.cloned.1.call-start = ((), (), s32[]{:S(2)}) async-start(), calls=%async_computation.11 | async-start | bytes 12779520
Sparse Core Ops, SparseCore 0:
  9.8 37.2 all-gather.6
  49.5 46.4 all-gather.4
  102.0 37.2 all-gather.8
  141.6 37.2 all-gather.10
  211.8 54.5 reduce-scatter.8
  268.8 57.7 reduce-scatter.6
  334.2 50.9 reduce-scatter.10
  390.1 156.4 reduce-scatter.12
where the time goes:
time: 560 us; the launch traced here: 556 us
  waiting for transfers between devices  466 us (83%)
  matrix products  37.2 us (7%)
  local copies, waits for them, and re-layouts  30.3 us (5%)
  between operations  14.2 us (3%)
  other arithmetic  8.58 us (2%)
    unnamed x9, waiting for transfers between devices  161 us
    reduce_scatter x1, waiting for transfers between devices, body(): lax.psum_scatter(key_part, 'row', scatter_dimension=1, tiled=True)  59.3 us
    reduce_scatter x1, waiting for transfers between devices, body(): lax.psum_scatter(value_part, 'row', scatter_dimension=1, tiled=True)  53.7 us
    all_gather x1, waiting for transfers between devices, body(): w_full = lax.all_gather(w_tile, 'row', axis=0, tiled=True)  48.9 us
    all_gather x1, waiting for transfers between devices, body(): lax.all_gather(values, 'row', axis=1, tiled=True)  39.6 us
    all_gather x1, waiting for transfers between devices, body(): lax.all_gather(inputs, 'col', axis=2, tiled=True).reshape(token_count, D)  37.2 us
    all_gather x1, waiting for transfers between devices, body(): lax.all_gather(keys, 'row', axis=1, tiled=True)  35.1 us
    reduce_scatter x1, waiting for transfers between devices, body(): lax.psum_scatter(input_part.reshape(seq_count, local_len, D), 'col', scat...  30.5 us
  transfers between devices with their start and end apart: 8, of which 8 were waited for; matrix products, arithmetic and copies ran while one was open for 5% of the time, Pallas kernels for 0%

commit v1 on v0

v1 whole, which is shorter than its diff:
```python
import functools

import jax
import jax.numpy as jnp
from jax import lax
from jax.experimental import pallas as pl
from jax.experimental.pallas import tpu as pltpu
from jax.sharding import PartitionSpec as P

HEAD_DIM = 128
ROWS, COLS, DEPTHS = 16, 4, 4
RING = ROWS // 2
TOK = 256
SEQ_TOK = 128
GROUP = 4
QW = 512
WIDTH = 768
KVW = 256
DCOL = 1024
TILE = 256
BF16, F32 = jnp.bfloat16, jnp.float32
SCALE = HEAD_DIM ** -0.5
EXP_SCALE = SCALE * 1.4426950408889634
NT = (((1,), (1,)), ((), ()))


class Net:
    def __init__(self, ssem, rsem):
        self.r = lax.axis_index("row")
        self.c = lax.axis_index("col")
        self.d = lax.axis_index("depth")
        self.z = self.r // 2
        self.core = lax.rem(self.r, 2)
        self.ssem, self.rsem = ssem, rsem
        self.count = 0
        self.sent = []
        self.peers = {
            "zr": {"row": lax.rem(self.r + 2, ROWS)},
            "zl": {"row": lax.rem(self.r + ROWS - 2, ROWS)},
            "sib": {"row": self.r + 1 - 2 * self.core},
            "yr": {"col": lax.rem(self.c + 1, COLS)},
            "yl": {"col": lax.rem(self.c + COLS - 1, COLS)},
            "xr": {"depth": lax.rem(self.d + 1, DEPTHS)},
            "xl": {"depth": lax.rem(self.d + DEPTHS - 1, DEPTHS)},
        }

    def barrier(self, names):
        bar = pltpu.get_barrier_semaphore()
        for name in names:
            pl.semaphore_signal(
                bar, inc=1, device_id=self.peers[name], device_id_type=pl.DeviceIdType.MESH
            )
        pl.semaphore_wait(bar, len(names))

    def send(self, src, dst, name):
        i = self.count
        self.count += 1
        copy = pltpu.make_async_remote_copy(
            src_ref=src,
            dst_ref=dst,
            send_sem=self.ssem.at[i],
            recv_sem=self.rsem.at[i],
            device_id=self.peers[name],
            device_id_type=pl.DeviceIdType.MESH,
        )
        copy.start()
        self.sent.append(copy)
        return copy

    def finish(self):
        for copy in self.sent:
            copy.wait_send()

    def zk(self, k):
        return lax.rem(self.z + k % RING, RING)


def ring_gather(net, slot, part_a, part_b, arrived):
    pend = {}
    pend["ra", 0] = net.send(slot(net.z, part_a), slot(net.z, part_a), "zr")
    pend["lb", 0] = net.send(slot(net.z, part_b), slot(net.z, part_b), "zl")
    pend["rb", 0] = net.send(slot(net.z, part_b), slot(net.z, part_b), "zr")
    pend["la", 0] = net.send(slot(net.z, part_a), slot(net.z, part_a), "zl")

    def step(s):
        for key, far in (("ra", 4), ("lb", 4), ("rb", 3), ("la", 3)):
            if s >= far:
                continue
            pend[key, s].wait_recv()
            k = -(s + 1) if key[0] == "r" else s + 1
            part = part_a if key[1] == "a" else part_b
            ref = slot(net.zk(k), part)
            if s + 1 < far:
                pend[key, s + 1] = net.send(ref, ref, "zr" if key[0] == "r" else "zl")
            arrived(s, k, key[1], ref)

    return step


def project_kernel(
    x_ref, wq_ref, wk_ref, wv_ref, qkv_ref, xt_out, wf_out, xf, wf, xt, ssem, rsem, lsem
):
    net = Net(ssem, rsem)
    c, d, core = net.c, net.d, net.core
    net.barrier(["zr", "zl", "sib", "yr", "yl", "xr", "xl"])

    own = wf.at[net.z, core]
    own[:, :, 0:QW] = wq_ref[...].reshape(4, 64, QW)
    own[:, :, QW : QW + 128] = wk_ref[...].reshape(4, 64, 128)
    own[:, :, QW + 128 :] = wv_ref[...].reshape(4, 64, 128)

    part_a, part_b = d, lax.rem(d + 1, DEPTHS)

    def slot(z, q):
        return wf.at[z, core, q]

    sib, cross = [], {}

    def arrived(s, k, half, ref):
        if half == "a":
            cross[k, "a"] = net.send(ref, ref, "xr")
        else:
            cross[k, "b"] = net.send(ref, ref, "xl")
        sib.append(net.send(ref, ref, "sib"))

    def crossed(s):
        for k in (-(s + 1), s + 1):
            for half in ("a", "b"):
                if s == 3 and (k > 0) != (half == "b"):
                    continue
                cross[k, half].wait_recv()
                q = lax.rem(d + (3 if half == "a" else 2), DEPTHS)
                ref = wf.at[net.zk(k), core, q]
                sib.append(net.send(ref, ref, "sib"))

    step = ring_gather(net, slot, part_a, part_b, arrived)
    ya_r = net.send(x_ref.at[0], xf.at[c, 0], "yr")
    yb_l = net.send(x_ref.at[1], xf.at[c, 1], "yl")
    yb_r = net.send(x_ref.at[1], xf.at[c, 1], "yr")
    ya_l = net.send(x_ref.at[0], xf.at[c, 0], "yl")
    sib.append(net.send(own, own, "sib"))
    xf[c] = x_ref[...]

    left, right = lax.rem(c + 3, COLS), lax.rem(c + 1, COLS)
    far = lax.rem(c + 2, COLS)

    def transpose(cc):
        for s in range(2):
            for k in range(DCOL // 128):
                xt[cc, k * 128 : (k + 1) * 128, s * 128 : (s + 1) * 128] = xf[
                    cc, s, :, k * 128 : (k + 1) * 128
                ].T

    step(0)
    transpose(c)
    step(1)
    ya_r.wait_recv()
    y2a = net.send(xf.at[left, 0], xf.at[left, 0], "yr")
    yb_l.wait_recv()
    y2b = net.send(xf.at[right, 1], xf.at[right, 1], "yl")
    crossed(0)
    step(2)
    crossed(1)
    yb_r.wait_recv()
    ya_l.wait_recv()
    step(3)
    crossed(2)
    transpose(left)
    transpose(right)
    crossed(3)
    y2a.wait_recv()
    y2b.wait_recv()
    transpose(far)
    for copy in sib:
        copy.wait_recv()
    out_x = pltpu.make_async_copy(xt, xt_out, lsem.at[0])
    out_w = pltpu.make_async_copy(wf, wf_out, lsem.at[1])
    out_x.start()
    out_w.start()
    acc = jnp.zeros((TOK, WIDTH), F32)
    for cc in range(COLS):
        acc = acc + jnp.dot(
            xf[cc].reshape(TOK, DCOL),
            wf[2 * cc : 2 * cc + 2].reshape(DCOL, WIDTH),
            preferred_element_type=F32,
        )
    qkv_ref[...] = acc.astype(BF16)
    net.finish()
    out_x.wait()
    out_w.wait()


def project(x, wq, wk, wv):
    vm = pl.BlockSpec(memory_space=pltpu.VMEM)
    hbm = pl.BlockSpec(memory_space=pl.ANY)
    n = 80
    return pl.pallas_call(
        project_kernel,
        name="project",
        out_shape=(
            jax.ShapeDtypeStruct((TOK, WIDTH), BF16),
            jax.ShapeDtypeStruct((COLS, DCOL, TOK), BF16),
            jax.ShapeDtypeStruct((RING, 2, 4, 64, WIDTH), BF16),
        ),
        in_specs=[vm] * 4,
        out_specs=(vm, hbm, hbm),
        scratch_shapes=[
            pltpu.VMEM((COLS, 2, SEQ_TOK, DCOL), BF16),
            pltpu.VMEM((RING, 2, 4, 64, WIDTH), BF16),
            pltpu.VMEM((COLS, DCOL, TOK), BF16),
            pltpu.SemaphoreType.DMA((n,)),
            pltpu.SemaphoreType.DMA((n,)),
            pltpu.SemaphoreType.DMA((2,)),
        ],
        compiler_params=pltpu.CompilerParams(
            collective_id=0, has_side_effects=True, vmem_limit_bytes=40 << 20
        ),
    )(x, wq, wk, wv)


def attend_kernel(
    qkv_ref, go_ref, rows_ref, kvb, qh, oh, prob, gprob, mblk, stat, dqt, part, fromsib, rin,
    ssem, rsem,
):
    net = Net(ssem, rsem)
    z, core, r = net.z, net.core, net.r
    for s in range(2):
        kvb[z, s, core] = qkv_ref[s * 128 : (s + 1) * 128, QW:]
        for h in range(GROUP):
            qh[s, h * 128 : (h + 1) * 128] = qkv_ref[
                s * 128 : (s + 1) * 128, h * 128 : (h + 1) * 128
            ]
            oh[s, h * 128 : (h + 1) * 128] = go_ref[s, :, h * 128 : (h + 1) * 128]
    net.barrier(["zr", "zl", "sib"])

    def slot(zz, half):
        return kvb.at[zz, half, core]

    sib = {}

    def arrived(s, k, half, ref):
        sib[k % RING, half] = net.send(ref, ref, "sib")

    sib[0, "a"] = net.send(slot(z, 0), slot(z, 0), "sib")
    sib[0, "b"] = net.send(slot(z, 1), slot(z, 1), "sib")
    step = ring_gather(net, slot, 0, 1, arrived)

    def scores(s, zz):
        kv = kvb[zz, s].reshape(2 * SEQ_TOK, KVW)
        st = lax.dot_general(kv[:, :HEAD_DIM], qh[s], NT, preferred_element_type=F32)
        dp = lax.dot_general(kv[:, HEAD_DIM:], oh[s], NT, preferred_element_type=F32)
        return st * EXP_SCALE, dp

    def first(s, carry):
        st, dp = scores(s, z)
        key = lax.broadcasted_iota(jnp.int32, (2 * SEQ_TOK, QW), 0)
        query = lax.rem(lax.broadcasted_iota(jnp.int32, (2 * SEQ_TOK, QW), 1), SEQ_TOK)
        st = jnp.where(key <= query + core * SEQ_TOK, st, -1e30)
        m = jnp.max(st, 0, keepdims=True)
        p = jnp.exp2(st - m)
        prob[z, s] = p
        gprob[z, s] = dp
        mblk[z, s] = m
        stat[s, 0:1] = m
        stat[s, 1:2] = jnp.sum(p, 0, keepdims=True)
        stat[s, 2:3] = jnp.sum(p * dp, 0, keepdims=True)
        return carry

    def more(zz):
        def one(s, carry):
            st, dp = scores(s, zz)
            old = stat[s, 0:1]
            m = jnp.maximum(old, jnp.max(st, 0, keepdims=True))
            p = jnp.exp2(st - m)
            fade = jnp.exp2(old - m)
            prob[zz, s] = p
            gprob[zz, s] = dp
            mblk[zz, s] = m
            stat[s, 0:1] = m
            stat[s, 1:2] = stat[s, 1:2] * fade + jnp.sum(p, 0, keepdims=True)
            stat[s, 2:3] = stat[s, 2:3] * fade + jnp.sum(p * dp, 0, keepdims=True)
            return carry

        @pl.when(zz < z)
        def _():
            lax.fori_loop(0, 2, one, 0)

    sib[0, "a"].wait_recv()
    sib[0, "b"].wait_recv()
    lax.fori_loop(0, 2, first, 0)
    part[...] = jnp.zeros_like(part)
    for s in range(4):
        step(s)
        for k in (-(s + 1), s + 1) if s < 3 else (4,):
            for half in ("a", "b"):
                sib[k % RING, half].wait_recv()
            more(net.zk(k))

    dqt[...] = jnp.zeros_like(dqt)
    for s in range(2):
        inv = 1.0 / stat[s, 1:2]
        stat[s, 3:4] = inv
        stat[s, 4:5] = stat[s, 2:3] * inv

    def back(zz, carry):
        for s in range(2):
            fac = jnp.exp2(mblk[zz, s] - stat[s, 0:1]) * stat[s, 3:4]
            p = prob[zz, s] * fac
            low = p.astype(BF16)
            ds = (p * (gprob[zz, s] - stat[s, 4:5])).astype(BF16)
            dv = jnp.dot(low, oh[s], preferred_element_type=F32)
            dk = jnp.dot(ds, qh[s], preferred_element_type=F32) * SCALE
            keys = kvb[zz, s].reshape(2 * SEQ_TOK, KVW)[:, :HEAD_DIM]
            dqt[s] += jnp.dot(keys.T, ds, preferred_element_type=F32)
            for co in range(2):
                part[zz, co, s, :, :HEAD_DIM] = dk[co * 128 : (co + 1) * 128].astype(BF16)
                part[zz, co, s, :, HEAD_DIM:] = dv[co * 128 : (co + 1) * 128].astype(BF16)
        return carry

    lax.fori_loop(0, z + 1, back, 0)

    def mine(zz, s):
        return part.at[zz, core, s]

    def fold(zz):
        part[zz, core] = (part[zz, core].astype(F32) + fromsib[zz].astype(F32)).astype(BF16)

    order = (4, 3, -3, 2, -2, 1, -1, 0)
    swap = {k: net.send(part.at[net.zk(k), 1 - core], fromsib.at[net.zk(k)], "sib") for k in order}
    for s in range(2):
        for h in range(GROUP):
            rows_ref[s * 128 : (s + 1) * 128, h * 128 : (h + 1) * 128] = (
                (dqt[s, :, h * 128 : (h + 1) * 128] * SCALE).T.astype(BF16)
            )
    got = {}

    def out(way, half, n):
        k = n if way == "r" else -n
        got[way, half, n] = net.send(
            mine(net.zk(k), half),
            rin.at[0 if way == "r" else 1, half, n - 1],
            "zr" if way == "r" else "zl",
        )

    def add(way, half, n, k):
        got[way, half, n].wait_recv()
        ref = mine(net.zk(k), half)
        src = rin.at[0 if way == "r" else 1, half, n - 1]
        ref[...] = (ref[...].astype(F32) + src[...].astype(F32)).astype(BF16)

    swap[4].wait_recv()
    fold(net.zk(4))
    out("r", 0, 4)
    out("l", 1, 4)
    for k in (3, -3):
        swap[k].wait_recv()
        fold(net.zk(k))
    out("r", 1, 3)
    out("l", 0, 3)
    add("r", 0, 4, 3)
    out("r", 0, 3)
    add("l", 1, 4, -3)
    out("l", 1, 3)
    for n in (2, 1):
        for k in (n, -n):
            swap[k].wait_recv()
            fold(net.zk(k))
        for way, half in (("r", 1), ("l", 0), ("r", 0), ("l", 1)):
            add(way, half, n + 1, n if way == "r" else -n)
            out(way, half, n)
    swap[0].wait_recv()
    for half in range(2):
        total = part[z, core, half].astype(F32) + fromsib[z, half].astype(F32)
        for way in ("r", "l"):
            got[way, half, 1].wait_recv()
        total = total + rin[0, half, 0].astype(F32) + rin[1, half, 0].astype(F32)
        rows_ref[half * 128 : (half + 1) * 128, QW:] = total.astype(BF16)
    net.finish()


def attend(qkv, go):
    vm = pl.BlockSpec(memory_space=pltpu.VMEM)
    n = 56
    return pl.pallas_call(
        attend_kernel,
        name="attend",
        out_shape=jax.ShapeDtypeStruct((TOK, WIDTH), BF16),
        in_specs=[vm] * 2,
        out_specs=vm,
        scratch_shapes=[
            pltpu.VMEM((RING, 2, 2, SEQ_TOK, KVW), BF16),
            pltpu.VMEM((2, QW, HEAD_DIM), BF16),
            pltpu.VMEM((2, QW, HEAD_DIM), BF16),
            pltpu.VMEM((RING, 2, 2 * SEQ_TOK, QW), F32),
            pltpu.VMEM((RING, 2, 2 * SEQ_TOK, QW), F32),
            pltpu.VMEM((RING, 2, 1, QW), F32),
            pltpu.VMEM((2, 8, QW), F32),
            pltpu.VMEM((2, HEAD_DIM, QW), F32),
            pltpu.VMEM((RING, 2, 2, SEQ_TOK, KVW), BF16),
            pltpu.VMEM((RING, 2, SEQ_TOK, KVW), BF16),
            pltpu.VMEM((2, 2, 4, SEQ_TOK, KVW), BF16),
            pltpu.SemaphoreType.DMA((n,)),
            pltpu.SemaphoreType.DMA((n,)),
        ],
        compiler_params=pltpu.CompilerParams(
            collective_id=1, has_side_effects=True, vmem_limit_bytes=48 << 20
        ),
    )(qkv, go)


def grads_kernel(
    rows_ref, xt_hbm, wf_hbm, gi_ref, gw_ref, wf, xt, gi, yin, dw, dwsib, xin, zin, fin,
    ssem, rsem, lsem,
):
    net = Net(ssem, rsem)
    z, core, c, d = net.z, net.core, net.c, net.d
    in_w = pltpu.make_async_copy(wf_hbm, wf, lsem.at[0])
    in_x = pltpu.make_async_copy(xt_hbm, xt, lsem.at[1])
    in_w.start()
    in_x.start()
    net.barrier(["zr", "zl", "sib", "yr", "yl", "xr", "xl"])
    in_w.wait()

    def input_part(cc):
        w = wf[pl.ds(2 * cc, 2)].reshape(DCOL, WIDTH)
        return lax.dot_general(rows_ref[...], w, NT, preferred_element_type=F32)

    def input_store(cc):
        gi[cc] = input_part(cc).astype(BF16).reshape(2, SEQ_TOK, DCOL)

    far, right, left = lax.rem(c + 2, COLS), lax.rem(c + 1, COLS), lax.rem(c + 3, COLS)
    input_store(far)
    y0 = net.send(gi.at[far, 0], yin.at[0], "yr")
    y1 = net.send(gi.at[far, 1], yin.at[1], "yl")
    input_store(right)
    y2 = net.send(gi.at[right, 1], yin.at[2], "yr")
    input_store(left)
    y3 = net.send(gi.at[left, 0], yin.at[3], "yl")
    in_x.wait()

    swap = {}

    def tile(k):
        zz = net.zk(k)
        for co in range(2):
            rows = xt[zz // 2, pl.ds(pl.multiple_of(lax.rem(zz, 2) * 512 + co * 256, 256), 256)]
            part = jnp.dot(rows, rows_ref[...], preferred_element_type=F32)
            dw[zz, co] = part.astype(BF16).reshape(4, 64, WIDTH)
        swap[k] = net.send(dw.at[zz, 1 - core], dwsib.at[zz], "sib")

    def add(ref, src):
        ref[...] = (ref[...].astype(F32) + src[...].astype(F32)).astype(BF16)

    quarter_a, quarter_b = d, lax.rem(d + 1, DEPTHS)
    cross = {}

    def fold(k):
        zz = net.zk(k)
        swap[k].wait_recv()
        add(dw.at[zz, core], dwsib.at[zz])
        ql, qr = lax.rem(d + 3, DEPTHS), lax.rem(d + 2, DEPTHS)
        cross[k, "a"] = net.send(dw.at[zz, core, ql], xin.at[zz, 0], "xl")
        cross[k, "b"] = net.send(dw.at[zz, core, qr], xin.at[zz, 1], "xr")

    def keep(k):
        zz = net.zk(k)
        cross[k, "a"].wait_recv()
        add(dw.at[zz, core, quarter_a], xin.at[zz, 0])
        cross[k, "b"].wait_recv()
        add(dw.at[zz, core, quarter_b], xin.at[zz, 1])

    got = {}

    def part_of(half):
        return quarter_a if half == 0 else quarter_b

    def out(way, half, n):
        k = n if way == "r" else -n
        got[way, half, n] = net.send(
            dw.at[net.zk(k), core, part_of(half)],
            zin.at[0 if way == "r" else 1, half, n - 1],
            "zr" if way == "r" else "zl",
        )

    def take(way, half, n, k):
        got[way, half, n].wait_recv()
        add(dw.at[net.zk(k), core, part_of(half)], zin.at[0 if way == "r" else 1, half, n - 1])

    tile(4)
    tile(3)
    tile(-3)
    fold(4)
    tile(2)
    tile(-2)
    fold(3)
    fold(-3)
    tile(1)
    tile(-1)
    keep(4)
    out("r", 0, 4)
    out("l", 1, 4)
    tile(0)
    fold(2)
    fold(-2)
    fold(1)
    fold(-1)
    fold(0)
    keep(3)
    out("r", 1, 3)
    keep(-3)
    out("l", 0, 3)
    y0.wait_recv()
    add(gi.at[right, 0], yin.at[0])
    y4 = net.send(gi.at[right, 0], yin.at[4], "yr")
    y1.wait_recv()
    add(gi.at[left, 1], yin.at[1])
    y5 = net.send(gi.at[left, 1], yin.at[5], "yl")
    take("r", 0, 4, 3)
    out("r", 0, 3)
    take("l", 1, 4, -3)
    out("l", 1, 3)
    own = input_part(c)
    for n in (2, 1):
        keep(n)
        keep(-n)
        for way, half in (("r", 1), ("l", 0), ("r", 0), ("l", 1)):
            take(way, half, n + 1, n if way == "r" else -n)
            out(way, half, n)
    keep(0)
    take("r", 1, 1, 0)
    take("l", 1, 1, 0)
    last = net.send(dw.at[z, core, quarter_b], fin, "xr")
    take("r", 0, 1, 0)
    take("l", 0, 1, 0)
    for copy in (y2, y3, y4, y5):
        copy.wait_recv()
    gi_ref[0] = (own[:SEQ_TOK] + yin[3].astype(F32) + yin[4].astype(F32)).astype(BF16)
    gi_ref[1] = (own[SEQ_TOK:] + yin[2].astype(F32) + yin[5].astype(F32)).astype(BF16)
    last.wait_recv()
    gw_ref[...] = dw[z, core, quarter_a].astype(F32) + fin[...].astype(F32)
    net.finish()


def grads(rows, xt, wf):
    vm = pl.BlockSpec(memory_space=pltpu.VMEM)
    hbm = pl.BlockSpec(memory_space=pl.ANY)
    n = 64
    return pl.pallas_call(
        grads_kernel,
        name="grads",
        out_shape=(
            jax.ShapeDtypeStruct((2, SEQ_TOK, DCOL), BF16),
            jax.ShapeDtypeStruct((64, WIDTH), F32),
        ),
        in_specs=[vm, hbm, hbm],
        out_specs=(vm, vm),
        scratch_shapes=[
            pltpu.VMEM((RING, 2, 4, 64, WIDTH), BF16),
            pltpu.VMEM((COLS, DCOL, TOK), BF16),
            pltpu.VMEM((COLS, 2, SEQ_TOK, DCOL), BF16),
            pltpu.VMEM((6, SEQ_TOK, DCOL), BF16),
            pltpu.VMEM((RING, 2, 4, 64, WIDTH), BF16),
            pltpu.VMEM((RING, 4, 64, WIDTH), BF16),
            pltpu.VMEM((RING, 2, 64, WIDTH), BF16),
            pltpu.VMEM((2, 2, 4, 64, WIDTH), BF16),
            pltpu.VMEM((64, WIDTH), BF16),
            pltpu.SemaphoreType.DMA((n,)),
            pltpu.SemaphoreType.DMA((n,)),
            pltpu.SemaphoreType.DMA((2,)),
        ],
        compiler_params=pltpu.CompilerParams(
            collective_id=2, has_side_effects=True, vmem_limit_bytes=48 << 20
        ),
    )(rows, xt, wf)


def body(inputs, w_query, w_key, w_value, grad_out):
    qkv, xt, wf = project(inputs, w_query, w_key, w_value)
    rows = attend(qkv, grad_out)
    grad_inputs, gw = grads(rows, xt, wf)
    return grad_inputs, gw[:, :QW], gw[:, QW : QW + 128], gw[:, QW + 128 :]


def solution(mesh):
    return jax.shard_map(
        body,
        mesh=mesh,
        in_specs=(
            P("depth", "row", "col"),
            P("row", "col"),
            P("row", "col"),
            P("row", "col"),
            P("depth", "row", "col"),
        ),
        out_specs=(
            P("depth", "row", "col"),
            P(("row", "depth"), "col"),
            P(("row", "depth"), "col"),
            P(("row", "depth"), "col"),
        ),
        check_vma=False,
    )
```

time: 560 us -> 121 us (0.22)
  waiting for transfers between devices: 466 us -> 0 us
  Pallas kernels: 0 us -> 111 us
  matrix products: 37.2 us -> 0 us
  local copies, waits for them, and re-layouts: 30.3 us -> 9.36 us
  between operations: 14.2 us -> 0.68 us
  other arithmetic: 8.58 us -> 0 us
    unnamed x9 -> x0, waiting for transfers between devices: 161 us -> none
    all_gather x4 -> x0, waiting for transfers between devices: 161 us -> none  [the longest x1 48.9 us: body(): w_full = lax.all_gather(w_tile, 'row', axis=0, tiled=True)]
    reduce_scatter x3 -> x0, waiting for transfers between devices: 144 us -> none  [the longest x1 59.3 us: body(): lax.psum_scatter(key_part, 'row', scatter_dimension=1, tiled=True)]
    pallas_call x0 -> x3, Pallas kernels: none -> 111 us  [the longest x1 38 us: grads(): pl.pallas_call(grads_kernel, name='grads', out_shape=(jax.ShapeDtypeStruc...]
    dot_general x15 -> x0, matrix products: 37.2 us -> none  [the longest x2 6.76 us: one_sequence(): jnp.einsum('qkgd,tkd->kgqt', cot_seq, value_seq, preferred_element_type=j...]
    unnamed x9 -> x13, local copies, waits for them, and re-layouts: 15.4 us -> 8.07 us
    dynamic_update_slice x10 -> x0, local copies, waits for them, and re-layouts: 5.96 us -> none  [body(): lax.map(one_sequence, (queries, keys_all, values_all, cot_heads))]
  transfers between devices with their start and end apart: 8 -> 0, of which waited for: 8 -> 0; matrix products, arithmetic and copies ran while one was open for 5% -> 0% of each run, Pallas kernels for 0% -> 0%
where the time goes in v1:
time: 121 us
  Pallas kernels  111 us (92%)
  local copies, waits for them, and re-layouts  9.36 us (8%)
    pallas_call x1, Pallas kernels, grads(): pl.pallas_call(grads_kernel, name='grads', out_shape=(jax.ShapeDtypeStruc...  38 us
    pallas_call x1, Pallas kernels, project(): pl.pallas_call(project_kernel, name='project', out_shape=(jax.ShapeDtypeS...  36.8 us
    pallas_call x1, Pallas kernels, attend(): pl.pallas_call(attend_kernel, name='attend', out_shape=jax.ShapeDtypeStru...  36.2 us
    unnamed x13, local copies, waits for them, and re-layouts  8.07 us

profile of v1, /device:TPU:1, one launch (start us, length us, event | category | flops | bytes accessed | tf_op | source)
XLA Modules:
  0.0 121.0 jit_solution(15257748112377370678)
XLA Ops:
  0.6 0.0 copy-start.1
  0.6 1.0 copy-done.1
  1.7 0.0 copy-start.2
  1.7 0.9 copy-done.2
  2.6 0.0 copy-start.4
  2.6 0.8 copy-done.4
  3.5 0.0 copy-start.5
  3.5 0.8 copy-done.5
  4.3 36.8 %project.1 = (bf16[256,768]{1,0:T(8,128)(2,1)S(1)}, bf16[4,1024,256]{2,1,0:T(8,128)(2,1)S(1)}, bf16[8,2,4,64,768]{4,3,2,1,0:T(8,128)(2,1)S(1)}) custom-call(bf16[2,128,1024]{2,1,0:T(8,128)(2,1)S(1)} %copy-done.1, bf16[256,512]{1,0:T(8,128)(2,1)S(1)} %copy-done.2, bf16[256,128]{1,0:T(8,128)(2,1)S(1)} %copy-done.4, bf16[256,128]{1,0:T(8,128)(2,1)S(1)} %copy-done.5), custom_call_target="tpu_custom_call" | custom-call | tf_op jit(solution)/shard_map/project/pallas_call | solution.py:197
  41.2 0.0 copy-start
  41.2 2.7 %copy-done = bf16[8,2,4,64,768]{4,3,2,1,0:T(8,128)(2,1)} copy-done((bf16[8,2,4,64,768]{4,3,2,1,0:T(8,128)(2,1)}, bf16[8,2,4,64,768]{4,3,2,1,0:T(8,128)(2,1)S(1)}, u32[]{:S(2)}) %copy-start) | copy-done | bytes 6291480
  43.8 0.0 copy-start.3
  43.8 0.9 copy-done.3
  44.8 36.2 %attend.1.rows_ref = bf16[256,768]{1,0:T(8,128)(2,1)S(1)} custom-call(bf16[256,768]{1,0:T(8,128)(2,1)S(1)} %get-tuple-element.9.qkv_ref, bf16[2,128,512]{2,1,0:T(8,128)(2,1)S(1)} %copy-done.3), custom_call_target="tpu_custom_call" | custom-call | tf_op jit(solution)/shard_map/attend/pallas_call | solution.py:384
  80.9 38.0 %grads.1 = (bf16[2,128,1024]{2,1,0:T(8,128)(2,1)S(1)}, f32[64,768]{1,0:T(8,128)S(1)}) custom-call(bf16[256,768]{1,0:T(8,128)(2,1)S(1)} %attend.1.rows_ref, bf16[4,1024,256]{2,1,0:T(8,128)(2,1)S(1)} %get-tuple-element.10.xt_hbm, bf16[8,2,4,64,768]{4,3,2,1,0:T(8,128)(2,1)} %copy-done), custom_call_target="tpu_custom_call" | custom-call | tf_op jit(solution)/shard_map/grads/pallas_call | solution.py:548
  118.9 0.6 fusion
  119.6 0.7 slice.9
  120.2 0.8 copy.10
Async XLA Ops:
  0.6 1.0 copy-start.1
  1.7 0.9 copy-start.2
  2.6 0.8 copy-start.4
  3.5 0.8 copy-start.5
  41.2 2.7 %copy-start = (bf16[8,2,4,64,768]{4,3,2,1,0:T(8,128)(2,1)}, bf16[8,2,4,64,768]{4,3,2,1,0:T(8,128)(2,1)S(1)}, u32[]{:S(2)}) copy-start(bf16[8,2,4,64,768]{4,3,2,1,0:T(8,128)(2,1)S(1)} %get-tuple-element.11.wf_hbm) | copy-start | bytes 18874372
  43.8 0.9 copy-start.3

commit v2 on v0

v2 whole, which is shorter than its diff:
```python
import functools

import jax
import jax.numpy as jnp
from jax import lax
from jax.experimental import pallas as pl
from jax.experimental.pallas import tpu as pltpu
from jax.sharding import PartitionSpec as P

HEAD_DIM = 128
ROWS, COLS, DEPTHS = 16, 4, 4
RING = ROWS // 2
TOK = 256
SEQ_TOK = 128
GROUP = 4
QW = 512
WIDTH = 768
KVW = 256
COPIES = 272
DCOL = 1024
TILE = 256
BF16, F32 = jnp.bfloat16, jnp.float32
SCALE = HEAD_DIM ** -0.5
EXP_SCALE = SCALE * 1.4426950408889634
NT = (((1,), (1,)), ((), ()))


class Net:
    def __init__(self, ssem, rsem):
        self.r = lax.axis_index("row")
        self.c = lax.axis_index("col")
        self.d = lax.axis_index("depth")
        self.z = self.r // 2
        self.core = lax.rem(self.r, 2)
        self.ssem, self.rsem = ssem, rsem
        self.count = 0
        self.sent = []
        self.peers = {
            "zr": {"row": lax.rem(self.r + 2, ROWS)},
            "zl": {"row": lax.rem(self.r + ROWS - 2, ROWS)},
            "sib": {"row": self.r + 1 - 2 * self.core},
            "yr": {"col": lax.rem(self.c + 1, COLS)},
            "yl": {"col": lax.rem(self.c + COLS - 1, COLS)},
            "yf": {"col": lax.rem(self.c + 2, COLS)},
            "xr": {"depth": lax.rem(self.d + 1, DEPTHS)},
            "xl": {"depth": lax.rem(self.d + DEPTHS - 1, DEPTHS)},
        }

    def barrier(self, names):
        bar = pltpu.get_barrier_semaphore()
        for name in names:
            pl.semaphore_signal(
                bar, inc=1, device_id=self.peers[name], device_id_type=pl.DeviceIdType.MESH
            )
        pl.semaphore_wait(bar, len(names))

    def send(self, src, dst, name):
        i = self.count
        self.count += 1
        copy = pltpu.make_async_remote_copy(
            src_ref=src,
            dst_ref=dst,
            send_sem=self.ssem.at[i],
            recv_sem=self.rsem.at[i],
            device_id=self.peers[name],
            device_id_type=pl.DeviceIdType.MESH,
        )
        copy.start()
        self.sent.append(copy)
        return copy

    def release(self, copies):
        for copy in copies:
            copy.wait_send()
        self.sent = [one for one in self.sent if all(one is not copy for copy in copies)]

    def finish(self):
        for copy in self.sent:
            copy.wait_send()

    def zk(self, k):
        return lax.rem(self.z + k % RING, RING)


def ring_gather(net, slot, part_a, part_b, arrived):
    pend = {}
    pend["ra", 0] = net.send(slot(net.z, part_a), slot(net.z, part_a), "zr")
    pend["lb", 0] = net.send(slot(net.z, part_b), slot(net.z, part_b), "zl")
    pend["rb", 0] = net.send(slot(net.z, part_b), slot(net.z, part_b), "zr")
    pend["la", 0] = net.send(slot(net.z, part_a), slot(net.z, part_a), "zl")

    def step(s):
        for key, far in (("ra", 4), ("lb", 4), ("rb", 3), ("la", 3)):
            if s >= far:
                continue
            pend[key, s].wait_recv()
            k = -(s + 1) if key[0] == "r" else s + 1
            part = part_a if key[1] == "a" else part_b
            ref = slot(net.zk(k), part)
            if s + 1 < far:
                pend[key, s + 1] = net.send(ref, ref, "zr" if key[0] == "r" else "zl")
            arrived(s, k, key[1], ref)

    return step


class WeightSum:
    def __init__(self, net, width, xt, rows, dw, dwsib, xin, zin, fin):
        self.net, self.width, self.xt, self.rows = net, width, xt, rows
        self.dw, self.dwsib, self.xin, self.zin, self.fin = dw, dwsib, xin, zin, fin
        self.quarter = (net.d, lax.rem(net.d + 1, DEPTHS))
        self.swap, self.cross, self.got = {}, {}, {}

    def tile(self, k):
        net, zz = self.net, self.net.zk(k)
        start = pl.multiple_of(lax.rem(zz, 2) * 512, 512)
        rows = self.xt[zz // 2, pl.ds(start, 512)]
        part = jnp.dot(rows, self.rows[...], preferred_element_type=F32)
        self.dw[zz] = part.astype(BF16).reshape(2, 4, 64, self.width)
        self.swap[k] = net.send(self.dw.at[zz, 1 - net.core], self.dwsib.at[zz], "sib")

    def fold(self, k):
        net, zz = self.net, self.net.zk(k)
        self.swap[k].wait_recv()
        add(self.dw.at[zz, net.core], self.dwsib.at[zz])
        ql, qr = lax.rem(net.d + 3, DEPTHS), lax.rem(net.d + 2, DEPTHS)
        self.cross[k, 0] = net.send(self.dw.at[zz, net.core, ql], self.xin.at[zz, 0], "xl")
        self.cross[k, 1] = net.send(self.dw.at[zz, net.core, qr], self.xin.at[zz, 1], "xr")

    def keep(self, k):
        zz = self.net.zk(k)
        for half in range(2):
            self.cross[k, half].wait_recv()
            add(self.dw.at[zz, self.net.core, self.quarter[half]], self.xin.at[zz, half])

    def out(self, way, half, n):
        net = self.net
        zz = net.zk(n if way == "r" else -n)
        self.got[way, half, n] = net.send(
            self.dw.at[zz, net.core, self.quarter[half]],
            self.zin.at[0 if way == "r" else 1, half, n - 1],
            "zr" if way == "r" else "zl",
        )

    def take(self, way, half, n):
        net = self.net
        self.got[way, half, n].wait_recv()
        zz = net.zk(n - 1 if way == "r" else 1 - n)
        add(
            self.dw.at[zz, net.core, self.quarter[half]],
            self.zin.at[0 if way == "r" else 1, half, n - 1],
        )

    def start(self):
        self.keep(4)
        self.out("r", 0, 4)
        self.out("l", 1, 4)

    def second(self):
        self.keep(3)
        self.out("r", 1, 3)
        self.keep(-3)
        self.out("l", 0, 3)

    def third(self):
        self.take("r", 0, 4)
        self.out("r", 0, 3)
        self.take("l", 1, 4)
        self.out("l", 1, 3)

    def later(self, n):
        self.keep(n)
        self.keep(-n)
        for way, half in (("r", 1), ("l", 0), ("r", 0), ("l", 1)):
            self.take(way, half, n + 1)
            self.out(way, half, n)

    def last(self):
        net = self.net
        self.keep(0)
        self.take("r", 1, 1)
        self.take("l", 1, 1)
        self.final = net.send(self.dw.at[net.z, net.core, self.quarter[1]], self.fin, "xr")
        self.take("r", 0, 1)
        self.take("l", 0, 1)

    def result(self):
        net = self.net
        self.final.wait_recv()
        return self.dw[net.z, net.core, self.quarter[0]].astype(F32) + self.fin[...].astype(F32)


def add(ref, src):
    ref[...] = (ref[...].astype(F32) + src[...].astype(F32)).astype(BF16)


def fused_kernel(
    x_hbm, wq_hbm, wk_hbm, wv_hbm, go_hbm, gi_ref, gq_ref, gk_ref, gv_ref,
    xf, wqf, wkf, xt, kvb, qh, oh, prob, gprob, mblk, stat, dqt, part, fromsib, rin,
    rq, rkv, wkv, yin, dwq, dwqsib, xqin, zqin, fqin, dwk, dwksib, xkin, zkin, fkin,
    ssem, rsem, lsem,
):
    net = Net(ssem, rsem)
    c, d, z, core = net.c, net.d, net.z, net.core
    left, right, far = lax.rem(c + 3, COLS), lax.rem(c + 1, COLS), lax.rem(c + 2, COLS)
    own_q, own_k = wqf.at[z, core], wkf.at[z, core]
    local = []

    def fetch(src, dst):
        copy = pltpu.make_async_copy(src, dst, lsem.at[len(local)])
        copy.start()
        local.append(copy)

    fetch(wk_hbm, own_k.at[:, :, pl.ds(0, 128)])
    fetch(wv_hbm, own_k.at[:, :, pl.ds(128, 128)])
    fetch(wq_hbm, own_q)
    fetch(x_hbm, xf.at[c])
    for s in range(2):
        for h in range(GROUP):
            fetch(go_hbm.at[s, :, pl.ds(h * 128, 128)], oh.at[s, pl.ds(h * 128, 128)])
    net.barrier(["zr", "zl", "sib", "yr", "yl", "yf", "xr", "xl"])
    for copy in local[:4]:
        copy.wait()

    class Spread:
        def __init__(self, full):
            self.full, self.sib, self.cross = full, [], {}
            own = full.at[z, core]
            self.step = ring_gather(
                net,
                lambda zz, q: full.at[zz, core, q],
                d,
                lax.rem(d + 1, DEPTHS),
                self.arrived,
            )
            self.sib.append(net.send(own, own, "sib"))

        def arrived(self, s, k, half, ref):
            self.cross[k, half] = net.send(ref, ref, "xr" if half == "a" else "xl")
            self.sib.append(net.send(ref, ref, "sib"))

        def crossed(self, s):
            for k in (-(s + 1), s + 1):
                for half in ("a", "b"):
                    if s == 3 and (k > 0) != (half == "b"):
                        continue
                    self.cross[k, half].wait_recv()
                    q = lax.rem(d + (3 if half == "a" else 2), DEPTHS)
                    ref = self.full.at[net.zk(k), core, q]
                    self.sib.append(net.send(ref, ref, "sib"))

        def complete(self):
            for copy in self.sib:
                copy.wait_recv()

    wk = Spread(wkf)
    ya_r = net.send(xf.at[c, 0], xf.at[c, 0], "yr")
    yb_l = net.send(xf.at[c, 1], xf.at[c, 1], "yl")
    yb_r = net.send(xf.at[c, 1], xf.at[c, 1], "yr")
    ya_l = net.send(xf.at[c, 0], xf.at[c, 0], "yl")
    wq = Spread(wqf)

    def transpose(cc):
        for s in range(2):
            for k in range(DCOL // 128):
                xt[cc, k * 128 : (k + 1) * 128, s * 128 : (s + 1) * 128] = xf[
                    cc, s, :, k * 128 : (k + 1) * 128
                ].T

    wk.step(0)
    transpose(c)
    wq.step(0)
    wk.step(1)
    wk.crossed(0)
    ya_r.wait_recv()
    y2a = net.send(xf.at[left, 0], xf.at[left, 0], "yr")
    yb_l.wait_recv()
    y2b = net.send(xf.at[right, 1], xf.at[right, 1], "yl")
    wq.step(1)
    wq.crossed(0)
    wk.step(2)
    wk.crossed(1)
    wq.step(2)
    wq.crossed(1)
    wk.step(3)
    wk.crossed(2)
    yb_r.wait_recv()
    ya_l.wait_recv()
    transpose(left)
    transpose(right)
    wq.step(3)
    wk.crossed(3)
    wq.crossed(2)
    wk.complete()

    def project(chunks, full, width):
        total = None
        for cc in chunks:
            w = full[pl.ds(2 * cc, 2)].reshape(DCOL, width)
            part = jnp.dot(xf[cc].reshape(TOK, DCOL), w, preferred_element_type=F32)
            total = part if total is None else total + part
        return total

    near = project((c, left, right), wkf, KVW)
    y2a.wait_recv()
    y2b.wait_recv()
    near = (near + project((far,), wkf, KVW)).astype(BF16)

    def slot(zz, half):
        return kvb.at[zz, half, core]

    kvb[z, 0, core] = near[:SEQ_TOK]
    kvb[z, 1, core] = near[SEQ_TOK:]
    kvsib = {}

    def kv_arrived(s, k, half, ref):
        kvsib[k % RING, half] = net.send(ref, ref, "sib")

    kvsib[0, "a"] = net.send(slot(z, 0), slot(z, 0), "sib")
    kvsib[0, "b"] = net.send(slot(z, 1), slot(z, 1), "sib")
    step = ring_gather(net, slot, 0, 1, kv_arrived)

    wkv_got = []
    for i, (cc, name) in enumerate(((far, "yf"), (right, "yr"), (left, "yl"))):
        wkv_got.append(net.send(wkf.at[pl.ds(2 * cc, 2), core], wkv.at[i, core], name))
    wq.crossed(3)
    step(0)
    wq.complete()
    query = project((c, left, right, far), wqf, QW).astype(BF16)
    for s in range(2):
        for h in range(GROUP):
            qh[s, h * 128 : (h + 1) * 128] = query[
                s * 128 : (s + 1) * 128, h * 128 : (h + 1) * 128
            ]
    for copy in local[4:]:
        copy.wait()
    transpose(far)
    net.release((ya_r, yb_l, yb_r, ya_l, y2a, y2b))

    def scores(s, zz):
        kv = kvb[zz, s].reshape(2 * SEQ_TOK, KVW)
        st = lax.dot_general(kv[:, :HEAD_DIM], qh[s], NT, preferred_element_type=F32)
        dp = lax.dot_general(kv[:, HEAD_DIM:], oh[s], NT, preferred_element_type=F32)
        return st * EXP_SCALE, dp

    def begin(s, carry):
        st, dp = scores(s, z)
        key = lax.broadcasted_iota(jnp.int32, (2 * SEQ_TOK, QW), 0)
        query_pos = lax.rem(lax.broadcasted_iota(jnp.int32, (2 * SEQ_TOK, QW), 1), SEQ_TOK)
        st = jnp.where(key <= query_pos + core * SEQ_TOK, st, -1e30)
        m = jnp.max(st, 0, keepdims=True)
        p = jnp.exp2(st - m)
        prob[z, s] = p
        gprob[z, s] = dp
        mblk[z, s] = m
        stat[s, 0:1] = m
        stat[s, 1:2] = jnp.sum(p, 0, keepdims=True)
        stat[s, 2:3] = jnp.sum(p * dp, 0, keepdims=True)
        return carry

    def more(zz):
        def one(s, carry):
            st, dp = scores(s, zz)
            old = stat[s, 0:1]
            m = jnp.maximum(old, jnp.max(st, 0, keepdims=True))
            p = jnp.exp2(st - m)
            fade = jnp.exp2(old - m)
            prob[zz, s] = p
            gprob[zz, s] = dp
            mblk[zz, s] = m
            stat[s, 0:1] = m
            stat[s, 1:2] = stat[s, 1:2] * fade + jnp.sum(p, 0, keepdims=True)
            stat[s, 2:3] = stat[s, 2:3] * fade + jnp.sum(p * dp, 0, keepdims=True)
            return carry

        @pl.when(zz < z)
        def _():
            lax.fori_loop(0, 2, one, 0)

    kvsib[0, "a"].wait_recv()
    kvsib[0, "b"].wait_recv()
    lax.fori_loop(0, 2, begin, 0)
    part[...] = jnp.zeros_like(part)
    dqt[...] = jnp.zeros_like(dqt)
    wkv_sib = []
    for s in range(4):
        if s:
            step(s)
        if s == 3:
            for i, copy in enumerate(wkv_got):
                copy.wait_recv()
                wkv_sib.append(net.send(wkv.at[i, core], wkv.at[i, core], "sib"))
        for k in (-(s + 1), s + 1) if s < 3 else (4,):
            for half in ("a", "b"):
                kvsib[k % RING, half].wait_recv()
            more(net.zk(k))

    for s in range(2):
        inv = 1.0 / stat[s, 1:2]
        stat[s, 3:4] = inv
        stat[s, 4:5] = stat[s, 2:3] * inv

    def back_block(zz):
        for s in range(2):
            fac = jnp.exp2(mblk[zz, s] - stat[s, 0:1]) * stat[s, 3:4]
            p = prob[zz, s] * fac
            low = p.astype(BF16)
            ds = (p * (gprob[zz, s] - stat[s, 4:5])).astype(BF16)
            dv = jnp.dot(low, oh[s], preferred_element_type=F32)
            dk = jnp.dot(ds, qh[s], preferred_element_type=F32) * SCALE
            keys = kvb[zz, s].reshape(2 * SEQ_TOK, KVW)[:, :HEAD_DIM]
            dqt[s] += jnp.dot(keys.T, ds, preferred_element_type=F32)
            for co in range(2):
                part[zz, co, s, :, :HEAD_DIM] = dk[co * 128 : (co + 1) * 128].astype(BF16)
                part[zz, co, s, :, HEAD_DIM:] = dv[co * 128 : (co + 1) * 128].astype(BF16)

    swap = {}

    def back(n):
        def one(i, carry):
            zz = lax.rem(z + n + i * (2 * RING - 2 * n), RING)

            @pl.when(zz <= z)
            def _():
                back_block(zz)

            return carry

        ks = (n, -n) if n % 4 else (n,)
        lax.fori_loop(0, len(ks), one, 0)
        for k in ks:
            swap[k] = net.send(part.at[net.zk(k), 1 - core], fromsib.at[net.zk(k)], "sib")

    def fold(k):
        swap[k].wait_recv()
        add(part.at[net.zk(k), core], fromsib.at[net.zk(k)])

    got = {}

    def out(way, half, n):
        got[way, half, n] = net.send(
            part.at[net.zk(n if way == "r" else -n), core, half],
            rin.at[0 if way == "r" else 1, half, n - 1],
            "zr" if way == "r" else "zl",
        )

    def take(way, half, n):
        got[way, half, n].wait_recv()
        add(
            part.at[net.zk(n - 1 if way == "r" else 1 - n), core, half],
            rin.at[0 if way == "r" else 1, half, n - 1],
        )

    def later(n):
        fold(n)
        fold(-n)
        for way, half in (("r", 1), ("l", 0), ("r", 0), ("l", 1)):
            take(way, half, n + 1)
            out(way, half, n)

    back(4)
    back(3)
    fold(4)
    out("r", 0, 4)
    out("l", 1, 4)
    back(2)
    fold(3)
    fold(-3)
    out("r", 1, 3)
    out("l", 0, 3)
    back(1)
    back(0)

    for s in range(2):
        for h in range(GROUP):
            rq[s * 128 : (s + 1) * 128, h * 128 : (h + 1) * 128] = (
                (dqt[s, :, h * 128 : (h + 1) * 128] * SCALE).T.astype(BF16)
            )

    def input_part(cc):
        w = wqf[pl.ds(2 * cc, 2)].reshape(DCOL, QW)
        return lax.dot_general(rq[...], w, NT, preferred_element_type=F32)

    def input_store(i, cc):
        xf[i] = input_part(cc).astype(BF16).reshape(2, SEQ_TOK, DCOL)

    to_far, to_right, to_left = xf.at[0], xf.at[1], xf.at[2]
    input_store(0, far)
    y0 = net.send(to_far.at[0], yin.at[0], "yr")
    y1 = net.send(to_far.at[1], yin.at[1], "yl")
    take("r", 0, 4)
    out("r", 0, 3)
    take("l", 1, 4)
    out("l", 1, 3)
    input_store(1, right)
    y2 = net.send(to_right.at[1], yin.at[2], "yr")
    input_store(2, left)
    y3 = net.send(to_left.at[0], yin.at[3], "yl")

    wsq = WeightSum(net, QW, xt, rq, dwq, dwqsib, xqin, zqin, fqin)
    wsk = WeightSum(net, KVW, xt, rkv.at[c], dwk, dwksib, xkin, zkin, fkin)
    for k in (4, 3, -3, 2, -2, 1, -1, 0):
        wsq.tile(k)
    for k in (4, 3, -3):
        wsq.fold(k)
    later(2)
    for k in (2, -2, 1, -1):
        wsq.fold(k)
    y0.wait_recv()
    add(to_right.at[0], yin.at[0])
    y4 = net.send(to_right.at[0], yin.at[4], "yr")
    y1.wait_recv()
    add(to_left.at[1], yin.at[1])
    y5 = net.send(to_left.at[1], yin.at[5], "yl")
    later(1)
    wsq.start()
    wsq.second()

    fold(0)
    for half in range(2):
        total = part[z, core, half].astype(F32)
        for way in range(2):
            got["rl"[way], half, 1].wait_recv()
            total = total + rin[way, half, 0].astype(F32)
        rkv[c, half * 128 : (half + 1) * 128] = total.astype(BF16)
    kv_sent = [net.send(rkv.at[c], rkv.at[c], name) for name in ("yf", "yr", "yl")]
    for k in (4, 3, -3, 2, -2, 1, -1, 0):
        wsk.tile(k)
    wsq.third()
    for k in (4, 3, -3, 2, -2, 1, -1):
        wsk.fold(k)
    wsq.fold(0)
    wsk.fold(0)
    total = input_part(c)
    wsq.later(2)
    wsk.start()
    wsk.second()
    wsq.later(1)
    wsk.third()
    wsk.later(2)
    wsq.last()
    wsk.later(1)
    for copy in wkv_sib:
        copy.wait_recv()

    def key_share(cc, w):
        return lax.dot_general(
            rkv[cc], w.reshape(DCOL, KVW), NT, preferred_element_type=F32
        )

    total = total + key_share(c, wkf[pl.ds(2 * c, 2)])
    for i, cc in enumerate((far, left, right)):
        kv_sent[i].wait_recv()
        w = jnp.stack([wkv[i, 0], wkv[i, 1]], 1)
        total = total + key_share(cc, w)
    wsk.last()
    for copy in (y2, y3, y4, y5):
        copy.wait_recv()
    gi_ref[0] = (total[:SEQ_TOK] + yin[3].astype(F32) + yin[4].astype(F32)).astype(BF16)
    gi_ref[1] = (total[SEQ_TOK:] + yin[2].astype(F32) + yin[5].astype(F32)).astype(BF16)
    gq_ref[...] = wsq.result()
    gkv = wsk.result()
    gk_ref[...] = gkv[:, :HEAD_DIM]
    gv_ref[...] = gkv[:, HEAD_DIM:]
    net.finish()
    assert net.count <= COPIES, net.count


def deliver_kernel(*refs):
    for src, dst in zip(refs[:4], refs[4:]):
        dst[...] = src[...]


def body(inputs, w_query, w_key, w_value, grad_out):
    vm = pl.BlockSpec(memory_space=pltpu.VMEM)
    hbm = pl.BlockSpec(memory_space=pltpu.HBM)
    results = pl.pallas_call(
        fused_kernel,
        name="fused",
        out_shape=(
            jax.ShapeDtypeStruct((2, SEQ_TOK, DCOL), BF16),
            jax.ShapeDtypeStruct((64, QW), F32),
            jax.ShapeDtypeStruct((64, HEAD_DIM), F32),
            jax.ShapeDtypeStruct((64, HEAD_DIM), F32),
        ),
        in_specs=[hbm] * 5,
        out_specs=(vm,) * 4,
        scratch_shapes=[
            pltpu.VMEM((COLS, 2, SEQ_TOK, DCOL), BF16),
            pltpu.VMEM((RING, 2, 4, 64, QW), BF16),
            pltpu.VMEM((RING, 2, 4, 64, KVW), BF16),
            pltpu.VMEM((COLS, DCOL, TOK), BF16),
            pltpu.VMEM((RING, 2, 2, SEQ_TOK, KVW), BF16),
            pltpu.VMEM((2, QW, HEAD_DIM), BF16),
            pltpu.VMEM((2, QW, HEAD_DIM), BF16),
            pltpu.VMEM((RING, 2, 2 * SEQ_TOK, QW), F32),
            pltpu.VMEM((RING, 2, 2 * SEQ_TOK, QW), F32),
            pltpu.VMEM((RING, 2, 1, QW), F32),
            pltpu.VMEM((2, 8, QW), F32),
            pltpu.VMEM((2, HEAD_DIM, QW), F32),
            pltpu.VMEM((RING, 2, 2, SEQ_TOK, KVW), BF16),
            pltpu.VMEM((RING, 2, SEQ_TOK, KVW), BF16),
            pltpu.VMEM((2, 2, 4, SEQ_TOK, KVW), BF16),
            pltpu.VMEM((TOK, QW), BF16),
            pltpu.VMEM((COLS, TOK, KVW), BF16),
            pltpu.VMEM((3, 2, 2, 4, 64, KVW), BF16),
            pltpu.VMEM((6, SEQ_TOK, DCOL), BF16),
            pltpu.VMEM((RING, 2, 4, 64, QW), BF16),
            pltpu.VMEM((RING, 4, 64, QW), BF16),
            pltpu.VMEM((RING, 2, 64, QW), BF16),
            pltpu.VMEM((2, 2, 4, 64, QW), BF16),
            pltpu.VMEM((64, QW), BF16),
            pltpu.VMEM((RING, 2, 4, 64, KVW), BF16),
            pltpu.VMEM((RING, 4, 64, KVW), BF16),
            pltpu.VMEM((RING, 2, 64, KVW), BF16),
            pltpu.VMEM((2, 2, 4, 64, KVW), BF16),
            pltpu.VMEM((64, KVW), BF16),
            pltpu.SemaphoreType.DMA((COPIES,)),
            pltpu.SemaphoreType.DMA((COPIES,)),
            pltpu.SemaphoreType.DMA((16,)),
        ],
        compiler_params=pltpu.CompilerParams(
            collective_id=0, has_side_effects=True, vmem_limit_bytes=58 << 20
        ),
    )(
        inputs,
        w_query.reshape(4, 64, QW),
        w_key.reshape(4, 64, HEAD_DIM),
        w_value.reshape(4, 64, HEAD_DIM),
        grad_out,
    )
    return pl.pallas_call(
        deliver_kernel,
        name="deliver",
        out_shape=[jax.ShapeDtypeStruct(one.shape, one.dtype) for one in results],
        in_specs=[vm] * 4,
        out_specs=[vm] * 4,
    )(*results)


def solution(mesh):
    return jax.shard_map(
        body,
        mesh=mesh,
        in_specs=(
            P("depth", "row", "col"),
            P("row", "col"),
            P("row", "col"),
            P("row", "col"),
            P("depth", "row", "col"),
        ),
        out_specs=(
            P("depth", "row", "col"),
            P(("row", "depth"), "col"),
            P(("row", "depth"), "col"),
            P(("row", "depth"), "col"),
        ),
        check_vma=False,
    )
```

time: 560 us -> 101 us (0.18)
  waiting for transfers between devices: 466 us -> 0 us
  Pallas kernels: 0 us -> 99.6 us
  matrix products: 37.2 us -> 0 us
  local copies, waits for them, and re-layouts: 30.3 us -> 0 us
  between operations: 14.2 us -> 0.64 us
  other arithmetic: 8.58 us -> 0 us
    unnamed x9 -> x0, waiting for transfers between devices: 161 us -> none
    all_gather x4 -> x0, waiting for transfers between devices: 161 us -> none  [the longest x1 48.9 us: body(): w_full = lax.all_gather(w_tile, 'row', axis=0, tiled=True)]
    reduce_scatter x3 -> x0, waiting for transfers between devices: 144 us -> none  [the longest x1 59.3 us: body(): lax.psum_scatter(key_part, 'row', scatter_dimension=1, tiled=True)]
    pallas_call x0 -> x2, Pallas kernels: none -> 99.6 us  [the longest x1 97.6 us: body(): pl.pallas_call(fused_kernel, name='fused', out_shape=(jax.ShapeDtypeStruc...]
    dot_general x15 -> x0, matrix products: 37.2 us -> none  [the longest x2 6.76 us: one_sequence(): jnp.einsum('qkgd,tkd->kgqt', cot_seq, value_seq, preferred_element_type=j...]
    unnamed x9 -> x0, local copies, waits for them, and re-layouts: 15.4 us -> none
    dynamic_update_slice x10 -> x0, local copies, waits for them, and re-layouts: 5.96 us -> none  [body(): lax.map(one_sequence, (queries, keys_all, values_all, cot_heads))]
  transfers between devices with their start and end apart: 8 -> 0, of which waited for: 8 -> 0; matrix products, arithmetic and copies ran while one was open for 5% -> 0% of each run, Pallas kernels for 0% -> 0%
where the time goes in v2:
time: 101 us; the launch traced here: 100 us
  Pallas kernels  99.6 us (99%)
    pallas_call x1, Pallas kernels, body(): pl.pallas_call(fused_kernel, name='fused', out_shape=(jax.ShapeDtypeStruc...  97.6 us

profile of v2, /device:TPU:1, one launch (start us, length us, event | category | flops | bytes accessed | tf_op | source)
XLA Modules:
  0.0 100.3 jit_solution(11349193048500589263)
XLA Ops:
  0.6 97.6 %fused.1 = (bf16[2,128,1024]{2,1,0:T(8,128)(2,1)}, f32[64,512]{1,0:T(8,128)}, f32[64,128]{1,0:T(8,128)}, f32[64,128]{1,0:T(8,128)}) custom-call(bf16[2,128,1024]{2,1,0:T(8,128)(2,1)} %x_hbm.1, bf16[4,64,512]{2,1,0:T(8,128)(2,1)} %bitcast.3, bf16[4,64,128]{2,1,0:T(8,128)(2,1)} %bitcast.4, bf16[4,64,128]{2,1,0:T(8,128)(2,1)} %bitcast.5, ...), custom_call_target="tpu_custom_call" | custom-call | tf_op jit(solution)/shard_map/fused/pallas_call | solution.py:577
  98.3 2.0 %deliver.1 = (bf16[2,128,1024]{2,1,0:T(8,128)(2,1)}, f32[64,512]{1,0:T(8,128)}, f32[64,128]{1,0:T(8,128)}, f32[64,128]{1,0:T(8,128)}) custom-call(bf16[2,128,1024]{2,1,0:T(8,128)(2,1)} %get-tuple-element.8.refs_0_, f32[64,512]{1,0:T(8,128)} %get-tuple-element.9.refs_1_, f32[64,128]{1,0:T(8,128)} %get-tuple-element.10.refs_2_, ...), custom_call_target="tpu_custom_call" | custom-call | tf_op jit(solution)/shard_map/deliver/pallas_call | solution.py:632

commit v3 on v2

--- a/solution.py
+++ b/solution.py
@@ -16,7 +16,7 @@
 QW = 512
 WIDTH = 768
 KVW = 256
-COPIES = 272
+COPIES = 288
 DCOL = 1024
 TILE = 256
 BF16, F32 = jnp.bfloat16, jnp.float32
@@ -44,7 +44,14 @@
             "yf": {"col": lax.rem(self.c + 2, COLS)},
             "xr": {"depth": lax.rem(self.d + 1, DEPTHS)},
             "xl": {"depth": lax.rem(self.d + DEPTHS - 1, DEPTHS)},
+            "xf": {"depth": lax.rem(self.d + 2, DEPTHS)},
         }
+        other = 1 - 2 * self.core
+        self.peers["zrs"] = {"row": lax.rem(self.r + 2 + other, ROWS)}
+        self.peers["zls"] = {"row": lax.rem(self.r + ROWS - 2 + other, ROWS)}
+        for k in (2, 3, 4, 5, 6):
+            self.peers["z%d" % k] = {"row": lax.rem(self.r + 2 * k, ROWS)}
+        self.peers["z1"], self.peers["z7"] = self.peers["zr"], self.peers["zl"]
 
     def barrier(self, names):
         bar = pltpu.get_barrier_semaphore()
@@ -82,7 +89,7 @@
         return lax.rem(self.z + k % RING, RING)
 
 
-def ring_gather(net, slot, part_a, part_b, arrived):
+def ring_gather(net, slot, part_a, part_b, arrived, both=None):
     pend = {}
     pend["ra", 0] = net.send(slot(net.z, part_a), slot(net.z, part_a), "zr")
     pend["lb", 0] = net.send(slot(net.z, part_b), slot(net.z, part_b), "zl")
@@ -99,95 +106,128 @@
             ref = slot(net.zk(k), part)
             if s + 1 < far:
                 pend[key, s + 1] = net.send(ref, ref, "zr" if key[0] == "r" else "zl")
+            if both is not None and s == 2 and far == 4:
+                both[key] = net.send(ref, ref, "zrs" if key[0] == "r" else "zls")
             arrived(s, k, key[1], ref)
 
     return step
 
 
 class WeightSum:
-    def __init__(self, net, width, xt, rows, dw, dwsib, xin, zin, fin):
-        self.net, self.width, self.xt, self.rows = net, width, xt, rows
-        self.dw, self.dwsib, self.xin, self.zin, self.fin = dw, dwsib, xin, zin, fin
-        self.quarter = (net.d, lax.rem(net.d + 1, DEPTHS))
-        self.swap, self.cross, self.got = {}, {}, {}
-
-    def tile(self, k):
-        net, zz = self.net, self.net.zk(k)
-        start = pl.multiple_of(lax.rem(zz, 2) * 512, 512)
-        rows = self.xt[zz // 2, pl.ds(start, 512)]
-        part = jnp.dot(rows, self.rows[...], preferred_element_type=F32)
-        self.dw[zz] = part.astype(BF16).reshape(2, 4, 64, self.width)
-        self.swap[k] = net.send(self.dw.at[zz, 1 - net.core], self.dwsib.at[zz], "sib")
+    def __init__(self, net, width, xt, xg, rows, acc, dw, dwsib):
+        self.net, self.width, self.xt, self.xg, self.rows = net, width, xt, xg, rows
+        self.acc, self.dw, self.dwsib = acc, dw, dwsib
+        self.swap = {}
+
+    def multiply(self, sources, first, last):
+        def group(g, carry):
+            at = pl.ds(2 * g, 2)
+            total = None if first else self.acc[at].reshape(256, self.width)
+            for i in sources:
+                x = self.xg[i - 1, at] if i else self.xt[at, :, self.net.d]
+                part = jnp.dot(x.reshape(256, TOK), self.rows[i], preferred_element_type=F32)
+                total = part if total is None else total + part
+            if last:
+                self.dw[at] = total.astype(BF16).reshape(2, 2, 64, self.width)
+            else:
+                self.acc[at] = total.reshape(2, 2, 64, self.width)
+            return carry
+
+        lax.fori_loop(0, RING // 2, group, 0)
+
+    def trade(self):
+        net = self.net
+        for k in (4, 3, -3, 2, -2, 1, -1, 0):
+            zz = net.zk(k)
+            self.swap[k] = net.send(self.dw.at[zz, 1 - net.core], self.dwsib.at[zz], "sib")
 
     def fold(self, k):
-        net, zz = self.net, self.net.zk(k)
+        zz = self.net.zk(k)
         self.swap[k].wait_recv()
-        add(self.dw.at[zz, net.core], self.dwsib.at[zz])
-        ql, qr = lax.rem(net.d + 3, DEPTHS), lax.rem(net.d + 2, DEPTHS)
-        self.cross[k, 0] = net.send(self.dw.at[zz, net.core, ql], self.xin.at[zz, 0], "xl")
-        self.cross[k, 1] = net.send(self.dw.at[zz, net.core, qr], self.xin.at[zz, 1], "xr")
-
-    def keep(self, k):
-        zz = self.net.zk(k)
-        for half in range(2):
-            self.cross[k, half].wait_recv()
-            add(self.dw.at[zz, self.net.core, self.quarter[half]], self.xin.at[zz, half])
+        add(self.dw.at[zz, self.net.core], self.dwsib.at[zz])
+
+
+class RingSum(WeightSum):
+    def __init__(self, zin, *rest):
+        super().__init__(*rest)
+        self.zin, self.got = zin, {}
+
+    def half(self, k, half):
+        return self.dw.at[self.net.zk(k), self.net.core, pl.ds(32 * half, 32)]
 
     def out(self, way, half, n):
-        net = self.net
-        zz = net.zk(n if way == "r" else -n)
-        self.got[way, half, n] = net.send(
-            self.dw.at[zz, net.core, self.quarter[half]],
+        self.got[way, half, n] = self.net.send(
+            self.half(n if way == "r" else -n, half),
             self.zin.at[0 if way == "r" else 1, half, n - 1],
             "zr" if way == "r" else "zl",
         )
 
     def take(self, way, half, n):
-        net = self.net
         self.got[way, half, n].wait_recv()
-        zz = net.zk(n - 1 if way == "r" else 1 - n)
         add(
-            self.dw.at[zz, net.core, self.quarter[half]],
+            self.half(n - 1 if way == "r" else 1 - n, half),
             self.zin.at[0 if way == "r" else 1, half, n - 1],
         )
 
     def start(self):
-        self.keep(4)
+        self.fold(4)
         self.out("r", 0, 4)
         self.out("l", 1, 4)
+        self.fold(3)
+        self.out("r", 1, 3)
+        self.fold(-3)
+        self.out("l", 0, 3)
 
     def second(self):
-        self.keep(3)
-        self.out("r", 1, 3)
-        self.keep(-3)
-        self.out("l", 0, 3)
-
-    def third(self):
         self.take("r", 0, 4)
         self.out("r", 0, 3)
         self.take("l", 1, 4)
         self.out("l", 1, 3)
 
     def later(self, n):
-        self.keep(n)
-        self.keep(-n)
+        self.fold(n)
+        self.fold(-n)
         for way, half in (("r", 1), ("l", 0), ("r", 0), ("l", 1)):
             self.take(way, half, n + 1)
             self.out(way, half, n)
 
-    def last(self):
+    def result(self):
+        self.fold(0)
+        net, parts = self.net, []
+        for half in range(2):
+            total = self.half(0, half)[...].astype(F32)
+            for way in range(2):
+                self.got["rl"[way], half, 1].wait_recv()
+                total = total + self.zin[way, half, 0].astype(F32)
+            parts.append(total)
+        return parts
+
+
+class DirectSum(WeightSum):
+    def __init__(self, zin, *rest):
+        super().__init__(*rest)
+        self.zin, self.got = zin, []
+
+    def start(self):
         net = self.net
-        self.keep(0)
-        self.take("r", 1, 1)
-        self.take("l", 1, 1)
-        self.final = net.send(self.dw.at[net.z, net.core, self.quarter[1]], self.fin, "xr")
-        self.take("r", 0, 1)
-        self.take("l", 0, 1)
+        for k in (4, 3, -3, 2, -2, 1, -1):
+            self.fold(k)
+            self.got.append(
+                net.send(
+                    self.dw.at[net.zk(k), net.core],
+                    self.zin.at[k % RING - 1],
+                    "z%d" % (k % RING),
+                )
+            )
+        self.fold(0)
 
     def result(self):
-        net = self.net
-        self.final.wait_recv()
-        return self.dw[net.z, net.core, self.quarter[0]].astype(F32) + self.fin[...].astype(F32)
+        total = self.dw[self.net.z, self.net.core].astype(F32)
+        for copy in self.got:
+            copy.wait_recv()
+        for i in range(RING - 1):
+            total = total + self.zin[i].astype(F32)
+        return total
 
 
 def add(ref, src):
@@ -196,8 +236,8 @@
 
 def fused_kernel(
     x_hbm, wq_hbm, wk_hbm, wv_hbm, go_hbm, gi_ref, gq_ref, gk_ref, gv_ref,
-    xf, wqf, wkf, xt, kvb, qh, oh, prob, gprob, mblk, stat, dqt, part, fromsib, rin,
-    rq, rkv, wkv, yin, dwq, dwqsib, xqin, zqin, fqin, dwk, dwksib, xkin, zkin, fkin,
+    xf, wqf, wkf, xt, kvb, qh, oh, prob, gprob, mblk, stat, dqt, part, fromsib, rin, rlate,
+    rq, rkx, rky, xg, wkv, yin, accq, dwq, dwqsib, zqin, acck, dwk, dwksib, zkin,
     ssem, rsem, lsem,
 ):
     net = Net(ssem, rsem)
@@ -218,7 +258,10 @@
     for s in range(2):
         for h in range(GROUP):
             fetch(go_hbm.at[s, :, pl.ds(h * 128, 128)], oh.at[s, pl.ds(h * 128, 128)])
-    net.barrier(["zr", "zl", "sib", "yr", "yl", "yf", "xr", "xl"])
+    net.barrier(
+        ["zr", "zl", "sib", "yr", "yl", "yf", "xr", "xl", "xf"]
+        + ["z2", "z3", "z4", "z5", "z6", "zrs", "zls"]
+    )
     for copy in local[:4]:
         copy.wait()
 
@@ -263,12 +306,24 @@
     def transpose(cc):
         for s in range(2):
             for k in range(DCOL // 128):
-                xt[cc, k * 128 : (k + 1) * 128, s * 128 : (s + 1) * 128] = xf[
-                    cc, s, :, k * 128 : (k + 1) * 128
-                ].T
-
+                xt[
+                    2 * cc + k // 4,
+                    (k % 4) // 2,
+                    2 * (k % 2) : 2 * (k % 2) + 2,
+                    :,
+                    s * 128 : (s + 1) * 128,
+                ] = xf[cc, s, :, k * 128 : (k + 1) * 128].T.reshape(2, 64, 128)
+
+    xg_got = [[], [], []]
+
+    def hand_round(cc):
+        for i, (n, name) in enumerate(((2, "xf"), (1, "xr"), (3, "xl"))):
+            at = pl.ds(2 * cc, 2)
+            quarter = lax.rem(d + n, DEPTHS)
+            xg_got[i].append(net.send(xt.at[at, :, quarter], xg.at[i, at], name))
+
+    transpose(c)
     wk.step(0)
-    transpose(c)
     wq.step(0)
     wk.step(1)
     wk.crossed(0)
@@ -314,15 +369,20 @@
     kvsib = {}
 
     def kv_arrived(s, k, half, ref):
-        kvsib[k % RING, half] = net.send(ref, ref, "sib")
+        if s < 3:
+            kvsib[k % RING, half] = net.send(ref, ref, "sib")
 
     kvsib[0, "a"] = net.send(slot(z, 0), slot(z, 0), "sib")
     kvsib[0, "b"] = net.send(slot(z, 1), slot(z, 1), "sib")
-    step = ring_gather(net, slot, 0, 1, kv_arrived)
+    kvboth = {}
+    step = ring_gather(net, slot, 0, 1, kv_arrived, kvboth)
 
     wkv_got = []
     for i, (cc, name) in enumerate(((far, "yf"), (right, "yr"), (left, "yl"))):
         wkv_got.append(net.send(wkf.at[pl.ds(2 * cc, 2), core], wkv.at[i, core], name))
+    transpose(far)
+    for cc in (c, left, right, far):
+        hand_round(cc)
     wq.crossed(3)
     step(0)
     wq.complete()
@@ -334,7 +394,6 @@
             ]
     for copy in local[4:]:
         copy.wait()
-    transpose(far)
     net.release((ya_r, yb_l, yb_r, ya_l, y2a, y2b))
 
     def scores(s, zz):
@@ -382,17 +441,15 @@
     lax.fori_loop(0, 2, begin, 0)
     part[...] = jnp.zeros_like(part)
     dqt[...] = jnp.zeros_like(dqt)
-    wkv_sib = []
     for s in range(4):
         if s:
             step(s)
-        if s == 3:
-            for i, copy in enumerate(wkv_got):
-                copy.wait_recv()
-                wkv_sib.append(net.send(wkv.at[i, core], wkv.at[i, core], "sib"))
         for k in (-(s + 1), s + 1) if s < 3 else (4,):
             for half in ("a", "b"):
-                kvsib[k % RING, half].wait_recv()
+                if s < 3:
+                    kvsib[k % RING, half].wait_recv()
+                else:
+                    kvboth["ra" if half == "a" else "lb"].wait_recv()
             more(net.zk(k))
 
     for s in range(2):
@@ -428,7 +485,7 @@
 
         ks = (n, -n) if n % 4 else (n,)
         lax.fori_loop(0, len(ks), one, 0)
-        for k in ks:
+        for k in ks if n % 4 or not n else ():
             swap[k] = net.send(part.at[net.zk(k), 1 - core], fromsib.at[net.zk(k)], "sib")
 
     def fold(k):
@@ -459,10 +516,12 @@
             out(way, half, n)
 
     back(4)
-    back(3)
-    fold(4)
     out("r", 0, 4)
     out("l", 1, 4)
+    late = []
+    for half, name in enumerate(("zrs", "zls")):
+        late.append(net.send(part.at[net.zk(4), 1 - core, half], rlate.at[half], name))
+    back(3)
     back(2)
     fold(3)
     fold(-3)
@@ -473,13 +532,19 @@
 
     for s in range(2):
         for h in range(GROUP):
-            rq[s * 128 : (s + 1) * 128, h * 128 : (h + 1) * 128] = (
+            rq[0, s * 128 : (s + 1) * 128, h * 128 : (h + 1) * 128] = (
                 (dqt[s, :, h * 128 : (h + 1) * 128] * SCALE).T.astype(BF16)
             )
 
+    top, low = pl.ds(0, SEQ_TOK), pl.ds(SEQ_TOK, SEQ_TOK)
+    rqa_r = net.send(rq.at[0, top], rq.at[2, top], "xr")
+    rqb_l = net.send(rq.at[0, low], rq.at[3, low], "xl")
+    rqb_r = net.send(rq.at[0, low], rq.at[2, low], "xr")
+    rqa_l = net.send(rq.at[0, top], rq.at[3, top], "xl")
+
     def input_part(cc):
         w = wqf[pl.ds(2 * cc, 2)].reshape(DCOL, QW)
-        return lax.dot_general(rq[...], w, NT, preferred_element_type=F32)
+        return lax.dot_general(rq[0], w, NT, preferred_element_type=F32)
 
     def input_store(i, cc):
         xf[i] = input_part(cc).astype(BF16).reshape(2, SEQ_TOK, DCOL)
@@ -488,80 +553,90 @@
     input_store(0, far)
     y0 = net.send(to_far.at[0], yin.at[0], "yr")
     y1 = net.send(to_far.at[1], yin.at[1], "yl")
-    take("r", 0, 4)
-    out("r", 0, 3)
-    take("l", 1, 4)
-    out("l", 1, 3)
+    for way, half, k in (("r", 0, 3), ("l", 1, -3)):
+        take(way, half, 4)
+        late[half].wait_recv()
+        add(part.at[net.zk(k), core, half], rlate.at[half])
+        out(way, half, 3)
     input_store(1, right)
     y2 = net.send(to_right.at[1], yin.at[2], "yr")
     input_store(2, left)
     y3 = net.send(to_left.at[0], yin.at[3], "yl")
 
-    wsq = WeightSum(net, QW, xt, rq, dwq, dwqsib, xqin, zqin, fqin)
-    wsk = WeightSum(net, KVW, xt, rkv.at[c], dwk, dwksib, xkin, zkin, fkin)
-    for k in (4, 3, -3, 2, -2, 1, -1, 0):
-        wsq.tile(k)
-    for k in (4, 3, -3):
-        wsq.fold(k)
+    wsq = RingSum(zqin, net, QW, xt, xg, rq, accq, dwq, dwqsib)
+    wsk = DirectSum(zkin, net, KVW, xt, xg, rkx, acck, dwk, dwksib)
+    wkv_sib = []
+    for i, copy in enumerate(wkv_got):
+        copy.wait_recv()
+        wkv_sib.append(net.send(wkv.at[i, core], wkv.at[i, core], "sib"))
+    wsq.multiply((0,), True, False)
     later(2)
-    for k in (2, -2, 1, -1):
-        wsq.fold(k)
+    rqa_r.wait_recv()
+    rqa_f = net.send(rq.at[2, top], rq.at[1, top], "xr")
+    rqb_l.wait_recv()
+    rqb_f = net.send(rq.at[3, low], rq.at[1, low], "xl")
+    later(1)
     y0.wait_recv()
     add(to_right.at[0], yin.at[0])
     y4 = net.send(to_right.at[0], yin.at[4], "yr")
     y1.wait_recv()
     add(to_left.at[1], yin.at[1])
     y5 = net.send(to_left.at[1], yin.at[5], "yl")
-    later(1)
-    wsq.start()
-    wsq.second()
-
+    total_own = input_part(c)
     fold(0)
     for half in range(2):
         total = part[z, core, half].astype(F32)
         for way in range(2):
             got["rl"[way], half, 1].wait_recv()
             total = total + rin[way, half, 0].astype(F32)
-        rkv[c, half * 128 : (half + 1) * 128] = total.astype(BF16)
-    kv_sent = [net.send(rkv.at[c], rkv.at[c], name) for name in ("yf", "yr", "yl")]
-    for k in (4, 3, -3, 2, -2, 1, -1, 0):
-        wsk.tile(k)
-    wsq.third()
-    for k in (4, 3, -3, 2, -2, 1, -1):
-        wsk.fold(k)
-    wsq.fold(0)
-    wsk.fold(0)
-    total = input_part(c)
+        rkx[0, half * 128 : (half + 1) * 128] = total.astype(BF16)
+    rkx_got = [net.send(rkx.at[0], rkx.at[i + 1], ("xf", "xr", "xl")[i]) for i in range(3)]
+    rky_got = [net.send(rkx.at[0], rky.at[i], ("yf", "yr", "yl")[i]) for i in range(3)]
+    wsk.multiply((0,), True, False)
+    for i in (1, 2):
+        for copy in xg_got[i]:
+            copy.wait_recv()
+    rqb_r.wait_recv()
+    rqa_l.wait_recv()
+    wsq.multiply((2, 3), False, False)
+    for copy in xg_got[0]:
+        copy.wait_recv()
+    rqa_f.wait_recv()
+    rqb_f.wait_recv()
+    wsq.multiply((1,), False, True)
+    wsq.trade()
+    wsq.start()
+    for copy in wkv_sib:
+        copy.wait_recv()
+    total = total_own
+    for i in (1, 2):
+        rkx_got[i].wait_recv()
+    wsk.multiply((2, 3), False, False)
+    wsq.second()
+    rkx_got[0].wait_recv()
+    wsk.multiply((1,), False, True)
+    wsk.trade()
     wsq.later(2)
     wsk.start()
-    wsk.second()
     wsq.later(1)
-    wsk.third()
-    wsk.later(2)
-    wsq.last()
-    wsk.later(1)
-    for copy in wkv_sib:
-        copy.wait_recv()
-
-    def key_share(cc, w):
-        return lax.dot_general(
-            rkv[cc], w.reshape(DCOL, KVW), NT, preferred_element_type=F32
-        )
-
-    total = total + key_share(c, wkf[pl.ds(2 * c, 2)])
-    for i, cc in enumerate((far, left, right)):
-        kv_sent[i].wait_recv()
-        w = jnp.stack([wkv[i, 0], wkv[i, 1]], 1)
-        total = total + key_share(cc, w)
-    wsk.last()
+
+    def key_share(rows, w):
+        return lax.dot_general(rows, w.reshape(DCOL, KVW), NT, preferred_element_type=F32)
+
+    total = total + key_share(rkx[0], wkf[pl.ds(2 * c, 2)])
+    for i in range(3):
+        rky_got[i].wait_recv()
+        total = total + key_share(rky[i], jnp.stack([wkv[i, 0], wkv[i, 1]], 1))
     for copy in (y2, y3, y4, y5):
         copy.wait_recv()
     gi_ref[0] = (total[:SEQ_TOK] + yin[3].astype(F32) + yin[4].astype(F32)).astype(BF16)
     gi_ref[1] = (total[SEQ_TOK:] + yin[2].astype(F32) + yin[5].astype(F32)).astype(BF16)
-    gq_ref[...] = wsq.result()
     gkv = wsk.result()
     gk_ref[...] = gkv[:, :HEAD_DIM]
     gv_ref[...] = gkv[:, HEAD_DIM:]
+    first, second = wsq.result()
+    gq_ref[:32] = first
+    gq_ref[32:] = second
     net.finish()
     assert net.count <= COPIES, net.count
 
@@ -589,7 +664,7 @@
             pltpu.VMEM((COLS, 2, SEQ_TOK, DCOL), BF16),
             pltpu.VMEM((RING, 2, 4, 64, QW), BF16),
             pltpu.VMEM((RING, 2, 4, 64, KVW), BF16),
-            pltpu.VMEM((COLS, DCOL, TOK), BF16),
+            pltpu.VMEM((RING, 2, 4, 64, TOK), BF16),
             pltpu.VMEM((RING, 2, 2, SEQ_TOK, KVW), BF16),
             pltpu.VMEM((2, QW, HEAD_DIM), BF16),
             pltpu.VMEM((2, QW, HEAD_DIM), BF16),
@@ -601,26 +676,27 @@
             pltpu.VMEM((RING, 2, 2, SEQ_TOK, KVW), BF16),
             pltpu.VMEM((RING, 2, SEQ_TOK, KVW), BF16),
             pltpu.VMEM((2, 2, 4, SEQ_TOK, KVW), BF16),
-            pltpu.VMEM((TOK, QW), BF16),
-            pltpu.VMEM((COLS, TOK, KVW), BF16),
+            pltpu.VMEM((2, SEQ_TOK, KVW), BF16),
+            pltpu.VMEM((DEPTHS, TOK, QW), BF16),
+            pltpu.VMEM((DEPTHS, TOK, KVW), BF16),
+            pltpu.VMEM((3, TOK, KVW), BF16),
+            pltpu.VMEM((3, RING, 2, 64, TOK), BF16),
             pltpu.VMEM((3, 2, 2, 4, 64, KVW), BF16),
             pltpu.VMEM((6, SEQ_TOK, DCOL), BF16),
-            pltpu.VMEM((RING, 2, 4, 64, QW), BF16),
-            pltpu.VMEM((RING, 4, 64, QW), BF16),
+            pltpu.VMEM((RING, 2, 64, QW), F32),
             pltpu.VMEM((RING, 2, 64, QW), BF16),
-            pltpu.VMEM((2, 2, 4, 64, QW), BF16),
-            pltpu.VMEM((64, QW), BF16),
-            pltpu.VMEM((RING, 2, 4, 64, KVW), BF16),
-            pltpu.VMEM((RING, 4, 64, KVW), BF16),
+            pltpu.VMEM((RING, 64, QW), BF16),
+            pltpu.VMEM((2, 2, 4, 32, QW), BF16),
+            pltpu.VMEM((RING, 2, 64, KVW), F32),
             pltpu.VMEM((RING, 2, 64, KVW), BF16),
-            pltpu.VMEM((2, 2, 4, 64, KVW), BF16),
-            pltpu.VMEM((64, KVW), BF16),
+            pltpu.VMEM((RING, 64, KVW), BF16),
+            pltpu.VMEM((RING - 1, 64, KVW), BF16),
             pltpu.SemaphoreType.DMA((COPIES,)),
             pltpu.SemaphoreType.DMA((COPIES,)),
             pltpu.SemaphoreType.DMA((16,)),
         ],
         compiler_params=pltpu.CompilerParams(
-            collective_id=0, has_side_effects=True, vmem_limit_bytes=58 << 20
+            collective_id=0, has_side_effects=True, vmem_limit_bytes=57 << 20
         ),
     )(
         inputs,

time: 101 us -> 97.3 us (0.963)
  Pallas kernels: 99.6 us -> 96.5 us
    pallas_call x1, Pallas kernels: 97.6 us -> 94.6 us  [body(): pl.pallas_call(fused_kernel, name='fused', out_shape=(jax.ShapeDtypeStruc...]
where the time goes in v3:
time: 97.3 us; the launch traced here: 97.2 us
  Pallas kernels  96.5 us (99%)
    pallas_call x1, Pallas kernels, body(): pl.pallas_call(fused_kernel, name='fused', out_shape=(jax.ShapeDtypeStruc...  94.6 us
    pallas_call x1, Pallas kernels, body(): pl.pallas_call(deliver_kernel, name='deliver', out_shape=[jax.ShapeDtypeS...  1.97 us

profile of v3, /device:TPU:1, one launch (start us, length us, event | category | flops | bytes accessed | tf_op | source)
XLA Modules:
  0.0 97.2 jit_solution(3928632962929825640)
XLA Ops:
  0.6 94.6 %fused.1 = (bf16[2,128,1024]{2,1,0:T(8,128)(2,1)}, f32[64,512]{1,0:T(8,128)}, f32[64,128]{1,0:T(8,128)}, f32[64,128]{1,0:T(8,128)}) custom-call(bf16[2,128,1024]{2,1,0:T(8,128)(2,1)} %x_hbm.1, bf16[4,64,512]{2,1,0:T(8,128)(2,1)} %bitcast.3, bf16[4,64,128]{2,1,0:T(8,128)(2,1)} %bitcast.4, bf16[4,64,128]{2,1,0:T(8,128)(2,1)} %bitcast.5, ...), custom_call_target="tpu_custom_call" | custom-call | tf_op jit(solution)/shard_map/fused/pallas_call | solution.py:652
  95.2 2.0 %deliver.1 = (bf16[2,128,1024]{2,1,0:T(8,128)(2,1)}, f32[64,512]{1,0:T(8,128)}, f32[64,128]{1,0:T(8,128)}, f32[64,128]{1,0:T(8,128)}) custom-call(bf16[2,128,1024]{2,1,0:T(8,128)(2,1)} %get-tuple-element.8.refs_0_, f32[64,512]{1,0:T(8,128)} %get-tuple-element.9.refs_1_, f32[64,128]{1,0:T(8,128)} %get-tuple-element.10.refs_2_, ...), custom_call_target="tpu_custom_call" | custom-call | tf_op jit(solution)/shard_map/deliver/pallas_call | solution.py:708

commit v4 on v3

--- a/solution.py
+++ b/solution.py
@@ -53,13 +53,13 @@
             self.peers["z%d" % k] = {"row": lax.rem(self.r + 2 * k, ROWS)}
         self.peers["z1"], self.peers["z7"] = self.peers["zr"], self.peers["zl"]
 
-    def barrier(self, names):
+    def greet(self, names):
         bar = pltpu.get_barrier_semaphore()
         for name in names:
             pl.semaphore_signal(
                 bar, inc=1, device_id=self.peers[name], device_id_type=pl.DeviceIdType.MESH
             )
-        pl.semaphore_wait(bar, len(names))
+        return len(names)
 
     def send(self, src, dst, name):
         i = self.count
@@ -243,6 +243,10 @@
     net = Net(ssem, rsem)
     c, d, z, core = net.c, net.d, net.z, net.core
     left, right, far = lax.rem(c + 3, COLS), lax.rem(c + 1, COLS), lax.rem(c + 2, COLS)
+    expected = net.greet(
+        ["zr", "zl", "sib", "yr", "yl", "yf", "xr", "xl", "xf"]
+        + ["z2", "z3", "z4", "z5", "z6", "zrs", "zls"]
+    )
     own_q, own_k = wqf.at[z, core], wkf.at[z, core]
     local = []
 
@@ -251,17 +255,11 @@
         copy.start()
         local.append(copy)
 
+    fetch(x_hbm, xf.at[c])
     fetch(wk_hbm, own_k.at[:, :, pl.ds(0, 128)])
     fetch(wv_hbm, own_k.at[:, :, pl.ds(128, 128)])
     fetch(wq_hbm, own_q)
-    fetch(x_hbm, xf.at[c])
-    for s in range(2):
-        for h in range(GROUP):
-            fetch(go_hbm.at[s, :, pl.ds(h * 128, 128)], oh.at[s, pl.ds(h * 128, 128)])
-    net.barrier(
-        ["zr", "zl", "sib", "yr", "yl", "yf", "xr", "xl", "xf"]
-        + ["z2", "z3", "z4", "z5", "z6", "zrs", "zls"]
-    )
+    pl.semaphore_wait(pltpu.get_barrier_semaphore(), expected)
     for copy in local[:4]:
         copy.wait()
 
@@ -322,6 +320,9 @@
             quarter = lax.rem(d + n, DEPTHS)
             xg_got[i].append(net.send(xt.at[at, :, quarter], xg.at[i, at], name))
 
+    for s in range(2):
+        for h in range(GROUP):
+            fetch(go_hbm.at[s, :, pl.ds(h * 128, 128)], oh.at[s, pl.ds(h * 128, 128)])
     transpose(c)
     wk.step(0)
     wq.step(0)
@@ -348,6 +349,8 @@
     wq.crossed(2)
     wk.complete()
 
+    settled = list(net.sent)
+
     def project(chunks, full, width):
         total = None
         for cc in chunks:
@@ -359,6 +362,8 @@
     near = project((c, left, right), wkf, KVW)
     y2a.wait_recv()
     y2b.wait_recv()
+    settled += [y2a, y2b]
+    settled = [one for one in net.sent if any(one is copy for copy in settled)]
     near = (near + project((far,), wkf, KVW)).astype(BF16)
 
     def slot(zz, half):
@@ -394,7 +399,6 @@
             ]
     for copy in local[4:]:
         copy.wait()
-    net.release((ya_r, yb_l, yb_r, ya_l, y2a, y2b))
 
     def scores(s, zz):
         kv = kvb[zz, s].reshape(2 * SEQ_TOK, KVW)
@@ -444,6 +448,8 @@
     for s in range(4):
         if s:
             step(s)
+        if s == 2:
+            net.release(settled)
         for k in (-(s + 1), s + 1) if s < 3 else (4,):
             for half in ("a", "b"):
                 if s < 3:
@@ -570,6 +576,8 @@
         copy.wait_recv()
         wkv_sib.append(net.send(wkv.at[i, core], wkv.at[i, core], "sib"))
     wsq.multiply((0,), True, False)
+    settled = [one for one in kvsib.values()] + list(kvboth.values())
+    net.release(settled)
     later(2)
     rqa_r.wait_recv()
     rqa_f = net.send(rq.at[2, top], rq.at[1, top], "xr")
@@ -616,6 +624,9 @@
     rkx_got[0].wait_recv()
     wsk.multiply((1,), False, True)
     wsk.trade()
+    net.release([one for n in got for one in (got[n],)])
+    net.release([one for copies in xg_got for one in copies] + wkv_got + wkv_sib + late)
+    net.release(list(swap.values()) + [y0, y1, y2, y3, y4, y5, rqa_r, rqb_l, rqb_r, rqa_l])
     wsq.later(2)
     wsk.start()
     wsq.later(1)

time: 97.3 us -> 96.9 us (level)
  no operation moved by 1% of the time
where the time goes in v4:
time: 96.9 us; the launch traced here: 96.8 us
  Pallas kernels  96.2 us (99%)
    pallas_call x1, Pallas kernels, body(): pl.pallas_call(fused_kernel, name='fused', out_shape=(jax.ShapeDtypeStruc...  94.2 us
    pallas_call x1, Pallas kernels, body(): pl.pallas_call(deliver_kernel, name='deliver', out_shape=[jax.ShapeDtypeS...  1.97 us

profile of v4, /device:TPU:1, one launch (start us, length us, event | category | flops | bytes accessed | tf_op | source)
XLA Modules:
  0.0 96.8 jit_solution(4447248600342083525)
XLA Ops:
  0.6 94.2 %fused.1 = (bf16[2,128,1024]{2,1,0:T(8,128)(2,1)}, f32[64,512]{1,0:T(8,128)}, f32[64,128]{1,0:T(8,128)}, f32[64,128]{1,0:T(8,128)}) custom-call(bf16[2,128,1024]{2,1,0:T(8,128)(2,1)} %x_hbm.1, bf16[4,64,512]{2,1,0:T(8,128)(2,1)} %bitcast.3, bf16[4,64,128]{2,1,0:T(8,128)(2,1)} %bitcast.4, bf16[4,64,128]{2,1,0:T(8,128)(2,1)} %bitcast.5, ...), custom_call_target="tpu_custom_call" | custom-call | tf_op jit(solution)/shard_map/fused/pallas_call | solution.py:663
  94.8 2.0 %deliver.1 = (bf16[2,128,1024]{2,1,0:T(8,128)(2,1)}, f32[64,512]{1,0:T(8,128)}, f32[64,128]{1,0:T(8,128)}, f32[64,128]{1,0:T(8,128)}) custom-call(bf16[2,128,1024]{2,1,0:T(8,128)(2,1)} %get-tuple-element.8.refs_0_, f32[64,512]{1,0:T(8,128)} %get-tuple-element.9.refs_1_, f32[64,128]{1,0:T(8,128)} %get-tuple-element.10.refs_2_, ...), custom_call_target="tpu_custom_call" | custom-call | tf_op jit(solution)/shard_map/deliver/pallas_call | solution.py:719

commit v5 on v3

--- a/solution.py
+++ b/solution.py
@@ -629,8 +629,10 @@
         total = total + key_share(rky[i], jnp.stack([wkv[i, 0], wkv[i, 1]], 1))
     for copy in (y2, y3, y4, y5):
         copy.wait_recv()
-    gi_ref[0] = (total[:SEQ_TOK] + yin[3].astype(F32) + yin[4].astype(F32)).astype(BF16)
-    gi_ref[1] = (total[SEQ_TOK:] + yin[2].astype(F32) + yin[5].astype(F32)).astype(BF16)
+    xf[3, 0] = (total[:SEQ_TOK] + yin[3].astype(F32) + yin[4].astype(F32)).astype(BF16)
+    xf[3, 1] = (total[SEQ_TOK:] + yin[2].astype(F32) + yin[5].astype(F32)).astype(BF16)
+    gi_out = pltpu.make_async_copy(xf.at[3], gi_ref, lsem.at[len(local)])
+    gi_out.start()
     gkv = wsk.result()
     gk_ref[...] = gkv[:, :HEAD_DIM]
     gv_ref[...] = gkv[:, HEAD_DIM:]
@@ -638,6 +640,7 @@
     gq_ref[:32] = first
     gq_ref[32:] = second
     net.finish()
+    gi_out.wait()
     assert net.count <= COPIES, net.count
 
 
@@ -659,7 +662,7 @@
             jax.ShapeDtypeStruct((64, HEAD_DIM), F32),
         ),
         in_specs=[hbm] * 5,
-        out_specs=(vm,) * 4,
+        out_specs=(hbm, vm, vm, vm),
         scratch_shapes=[
             pltpu.VMEM((COLS, 2, SEQ_TOK, DCOL), BF16),
             pltpu.VMEM((RING, 2, 4, 64, QW), BF16),

time: 97.3 us -> 97.1 us (level)
  no operation moved by 1% of the time
where the time goes in v5:
time: 97.1 us; the launch traced here: 97 us
  Pallas kernels  96.4 us (99%)
    pallas_call x1, Pallas kernels, body(): pl.pallas_call(fused_kernel, name='fused', out_shape=(jax.ShapeDtypeStruc...  94.4 us
    pallas_call x1, Pallas kernels, body(): pl.pallas_call(deliver_kernel, name='deliver', out_shape=[jax.ShapeDtypeS...  1.97 us

profile of v5, /device:TPU:1, one launch (start us, length us, event | category | flops | bytes accessed | tf_op | source)
XLA Modules:
  0.0 97.0 jit_solution(7486952335905642190)
XLA Ops:
  0.6 94.4 %fused.1 = (bf16[2,128,1024]{2,1,0:T(8,128)(2,1)}, f32[64,512]{1,0:T(8,128)}, f32[64,128]{1,0:T(8,128)}, f32[64,128]{1,0:T(8,128)}) custom-call(bf16[2,128,1024]{2,1,0:T(8,128)(2,1)} %x_hbm.1, bf16[4,64,512]{2,1,0:T(8,128)(2,1)} %bitcast.3, bf16[4,64,128]{2,1,0:T(8,128)(2,1)} %bitcast.4, bf16[4,64,128]{2,1,0:T(8,128)(2,1)} %bitcast.5, ...), custom_call_target="tpu_custom_call" | custom-call | tf_op jit(solution)/shard_map/fused/pallas_call | solution.py:655
  95.0 2.0 %deliver.1 = (bf16[2,128,1024]{2,1,0:T(8,128)(2,1)}, f32[64,512]{1,0:T(8,128)}, f32[64,128]{1,0:T(8,128)}, f32[64,128]{1,0:T(8,128)}) custom-call(bf16[2,128,1024]{2,1,0:T(8,128)(2,1)} %get-tuple-element.8.refs_0_, f32[64,512]{1,0:T(8,128)} %get-tuple-element.9.refs_1_, f32[64,128]{1,0:T(8,128)} %get-tuple-element.10.refs_2_, ...), custom_call_target="tpu_custom_call" | custom-call | tf_op jit(solution)/shard_map/deliver/pallas_call | solution.py:711
